TPU v7x, 128 devices: a whole 4x4x4 slice. The times are simulated.
128 devices in a mesh: row: 8 (over y, x_lo), col: 8 (over x_hi, z), dir: 2 (over core).
Axes of the slice: x: 4 (x_hi: 2, x_lo: 2; x = x_hi * 2 + x_lo), y: 4, z: 4, core: 2. Of those that a mesh axis runs over, the one named last changes fastest.
Arguments:
- vis: bfloat16 [2, 8, 2048, 2048], P(None, None, 'row', 'col'), may hold values from -80 to 80, as said below
- model: bfloat16 [4, 2, 8, 2048, 2048], P('dir', None, None, 'row', 'col'), may hold values from -9 to 9, as said below
- gains: float32 [2, 4, 2, 2048], P(None, 'dir', None, 'col'), may hold values from -4 to 4
- channel_interval_index: int32 [4, 8], replicated, may hold values from 0 to 1
- antenna_usable_mask: int32 [8, 2048], replicated, may hold values 0 or 1
Outputs:
- gains_new: float32 [2, 4, 2, 2048], P(None, 'dir', None, 'col')
- residual: float32 [2, 8, 2048, 2048], P(None, 'dir', 'row', 'col')
Inputs may be any that keep to these rules, and one draw needn't show every extreme that they name: For every channel vis is Hermitian in its last two dimensions: vis[0, c, p, q] = vis[0, c, q, p] and vis[1, c, p, q] = -vis[1, c, q, p]. For every direction and channel model is Hermitian in its last two dimensions: model[d, 0, c, p, q] = model[d, 0, c, q, p] and model[d, 1, c, p, q] = -model[d, 1, c, q, p].
All inputs are finite; a program needn't handle non-finite values.
Results may differ from a plain program's by a relative error of at most 0.0006.
Values may be sent and summed in bfloat16 or wider, within the bound.
A program may use at most 64 MiB of HBM per device.

v0:
```python
import jax
import jax.numpy as jnp
from jax import lax
from jax.sharding import PartitionSpec as P

ITERS = 2


def from_root(value, axis, source):
    kept = jnp.where(lax.axis_index(axis) == source, value, 0).astype(value.dtype)
    return lax.psum(kept, axis)


def expand(gain_set, onehot):
    return jnp.einsum("dck,xdkp->xdcp", onehot, gain_set, precision=lax.Precision.HIGHEST)


def collect(values, onehot):
    return jnp.einsum("dck,xdcp->xdkp", onehot, values, precision=lax.Precision.HIGHEST)


def collect_den(values, onehot):
    return jnp.einsum("dck,dcp->dkp", onehot, values, precision=lax.Precision.HIGHEST)


def predict(model_re, model_im, rows_re, rows_im, cols_re, cols_im):
    left_re = rows_re[:, :, None] * model_re - rows_im[:, :, None] * model_im
    left_im = rows_re[:, :, None] * model_im + rows_im[:, :, None] * model_re
    pred_re = left_re * cols_re[:, None, :] + left_im * cols_im[:, None, :]
    pred_im = left_im * cols_re[:, None, :] - left_re * cols_im[:, None, :]
    return (pred_re, pred_im)


def refresh(current, numer, denom):
    fresh = (numer + current) / (denom[None] + 1.0)
    return 0.5 * (fresh + current)


def sum_terms(terms):
    total = terms[0]
    for entry in terms[1:]:
        total = total + entry
    return total


def body(vis, model, gains, channel_interval_index, antenna_usable_mask):
    row_at = lax.axis_index("row")
    col_at = lax.axis_index("col")
    dir_at = lax.axis_index("dir")
    dir_count = lax.axis_size("dir")
    rows_here = vis.shape[2]
    cols_here = vis.shape[3]
    chan_share = vis.shape[1] // dir_count
    dir_dev = model.shape[0]
    groups = gains.shape[2]
    onehot_all = (
        channel_interval_index[:, :, None] == jnp.arange(groups, dtype=jnp.int32)[None, None, :]
    ).astype(jnp.float32)
    flag_mask = antenna_usable_mask.astype(jnp.float32)
    gains_cols = gains
    onehot = lax.dynamic_slice_in_dim(onehot_all, dir_at * dir_dev, dir_dev, 0)
    flags_rows = lax.dynamic_slice_in_dim(flag_mask, row_at * rows_here, rows_here, 1)
    flags_cols = lax.dynamic_slice_in_dim(flag_mask, col_at * cols_here, cols_here, 1)
    row_index = row_at * rows_here + jnp.arange(rows_here, dtype=jnp.int32)
    col_index = col_at * cols_here + jnp.arange(cols_here, dtype=jnp.int32)
    offdiag = (row_index[:, None] != col_index[None, :]).astype(jnp.float32)
    weight = flags_rows[:, :, None] * flags_cols[:, None, :] * offdiag[None]
    visibility_real = vis[0].astype(jnp.float32)
    vis_im = vis[1].astype(jnp.float32)
    held = model.shape[0]
    gains_rows = from_root(gains_cols, "col", row_at)

    def residual_of(rows_full, cols_full):
        preds = []
        for which in range(held):
            preds.append(
                predict(
                    model[which, 0].astype(jnp.float32),
                    model[which, 1].astype(jnp.float32),
                    rows_full[0, which],
                    rows_full[1, which],
                    cols_full[0, which],
                    cols_full[1, which],
                )
            )
        partial_value = jnp.stack(
            [sum_terms([entry[0] for entry in preds]), sum_terms([entry[1] for entry in preds])]
        )
        partial_value = lax.psum(partial_value, "dir")
        return (visibility_real - partial_value[0], vis_im - partial_value[1], preds)

    for sweep in range(ITERS):
        rows_full = expand(gains_rows, onehot)
        cols_full = expand(gains_cols, onehot)
        res_re, res_im, preds = residual_of(rows_full, cols_full)
        row_num_re, row_numerator_imaginary, row_den = ([], [], [])
        for which in range(held):
            data_re = res_re + preds[which][0]
            data_im = res_im + preds[which][1]
            model_re = model[which, 0].astype(jnp.float32)
            model_im = model[which, 1].astype(jnp.float32)
            cols_re = cols_full[0, which][:, None, :]
            cols_im = cols_full[1, which][:, None, :]
            pair_re = model_re * cols_re + model_im * cols_im
            pair_im = model_im * cols_re - model_re * cols_im
            row_num_re.append(jnp.sum(weight * (data_re * pair_re + data_im * pair_im), axis=2))
            row_numerator_imaginary.append(
                jnp.sum(weight * (data_im * pair_re - data_re * pair_im), axis=2)
            )
            row_den.append(jnp.sum(weight * (pair_re * pair_re + pair_im * pair_im), axis=2))
        numer_rows = collect(
            jnp.stack([jnp.stack(row_num_re), jnp.stack(row_numerator_imaginary)]), onehot
        )
        denom_rows = collect_den(jnp.stack(row_den), onehot)
        numer_rows, denom_rows = lax.psum((numer_rows, denom_rows), "col")
        gains_rows = refresh(gains_rows, numer_rows, denom_rows)
        gains_cols = from_root(gains_rows, "row", col_at)
    res_re, res_im, preds = residual_of(expand(gains_rows, onehot), expand(gains_cols, onehot))
    residual = jnp.stack([res_re, res_im])
    residual = lax.dynamic_slice_in_dim(residual, dir_at * chan_share, chan_share, 1)
    return (gains_cols, residual)


def solution(mesh):
    placed = (
        P(None, None, "row", "col"),
        P("dir", None, None, "row", "col"),
        P(None, "dir", None, "col"),
        P(),
        P(),
    )
    return jax.shard_map(
        body,
        mesh=mesh,
        in_specs=placed,
        out_specs=(P(None, "dir", None, "col"), P(None, "dir", "row", "col")),
        check_vma=False,
    )
```

profile of v0, /device:TPU:1, one launch (start us, length us, event | category | flops | bytes accessed | tf_op | source)
XLA Modules:
  0.0 305.2 jit_solution(10494501126755759799)
XLA Ops:
  7.2 0.7 broadcast_select_fusion
  7.9 22.8 %psum.70 = f32[2,2,2,256]{3,2,0,1:T(2,128)S(1)} all-reduce(f32[2,2,2,256]{3,2,0,1:T(2,128)S(1)} %broadcast_select_fusion), channel_id=1, replica_groups=mesh['row'=8,'col'=8,'dir'=2] {'col'}, use_global_device_ids=true, to_apply=%region_0.1 | all-reduce | flops 2048 | bytes 16384 | tf_op jit(solution)/shard_map/psum | solution.py:11
  30.7 0.9 convolution_bitcast_fusion.4
  31.9 4.3 %add_add_fusion.6 = (f32[1,8,256,256]{3,2,1,0:T(8,128)S(1)}, f32[1,8,256,256]{3,2,1,0:T(8,128)S(1)}) fusion(f32[8,256]{1,0:T(8,128)S(1)} %get-tuple-element.59, f32[8,256]{1,0:T(8,128)S(1)} %get-tuple-element.60, f32[8,256]{1,0:T(8,128)S(1)} %get-tuple-element.55, f32[8,256]{1,0:T(8,128)S(1)} %get-tuple-element.56, f32[8,256]{1,0:T(8,128)S(1)} %get-tuple-element.61, ...), kind=kLoop, calls=%fused_computation.133 | loop fusion | flops 15728640 | bytes 8454144 | tf_op jit(solution)/shard_map/add | solution.py:42
  36.2 2.4 pad_maximum_fusion
  38.7 0.8 copy-done.6
  39.6 34.4 %all-reduce.6.cloned.1.call-done = f32[2,8,256,256]{3,2,1,0:T(8,128)} async-done(((f32[2,8,256,256]{3,2,1,0:T(8,128)}), f32[2,8,256,256]{3,2,1,0:T(8,128)}) %all-reduce.6.cloned.1.call-update) | async-done | bytes 4194320 | tf_op jit(solution)/shard_map/psum | solution.py:89
  74.0 8.1 %multiply_reduce_fusion.7 = (f32[8,256]{1,0:T(8,128)S(1)}, f32[8,256]{1,0:T(8,128)S(1)}, f32[8,256]{1,0:T(8,128)S(1)}, f32[8,256]{1,0:T(8,128)S(1)}) fusion(f32[8,256]{1,0:T(8,128)S(1)} %get-tuple-element.61, f32[8,256]{1,0:T(8,128)S(1)} %get-tuple-element.58, f32[256,256]{1,0:T(8,128)S(1)} %compare_convert_fusion, f32[8,256]{1,0:T(8,128)S(1)} %get-tuple-element.37, ...), kind=kLoop, calls=%fused_computation.123 | loop fusion | flops 29351936 | bytes 10846208 | tf_op jit(solution)/shard_map/reduce_sum | solution.py:110
  82.3 4.0 %multiply_reduce_fusion.11 = (f32[8,256]{1,0:T(8,128)S(1)}, f32[8,256]{1,0:T(8,128)S(1)}) fusion(f32[2,8,256,256]{3,2,1,0:T(8,128)S(1)} %copy-done.4, f32[8,256]{1,0:T(8,128)S(1)} %get-tuple-element.61, f32[8,256]{1,0:T(8,128)S(1)} %get-tuple-element.58, f32[8,256]{1,0:T(8,128)S(1)} %get-tuple-element.57, f32[8,256]{1,0:T(8,128)S(1)} %get-tuple-element.54, ...), kind=kLoop, calls=%fused_computation.129 | loop fusion | flops 19918848 | bytes 8716288 | tf_op jit(solution)/shard_map/reduce_sum | solution.py:106
  86.5 34.7 %all-reduce.1 = (f32[2,2,2,256]{3,2,0,1:T(2,128)S(1)}, f32[2,2,256]{2,1,0:T(2,128)S(1)}) all-reduce(f32[2,2,2,256]{3,2,0,1:T(2,128)S(1)} %convolution_bitcast_fusion.7, f32[2,2,256]{2,1,0:T(2,128)S(1)} %fusion.95), channel_id=1, replica_groups=mesh['row'=8,'col'=8,'dir'=2] {'col'}, use_global_device_ids=true, to_apply=%region_6.7 | all-reduce | flops 3072 | bytes 24576 | tf_op jit(solution)/shard_map/psum | solution.py:115
  121.2 15.4 %psum.74 = f32[2,2,2,256]{3,2,0,1:T(2,128)S(1)} all-reduce(f32[2,2,2,256]{3,2,0,1:T(2,128)S(1)} %get-tuple-element.22), channel_id=1, replica_groups=mesh['row'=8,'col'=8,'dir'=2] {'row'}, use_global_device_ids=true, to_apply=%region_10.11 | all-reduce | flops 2048 | bytes 16384 | tf_op jit(solution)/shard_map/psum | solution.py:11
  137.0 4.3 %add_add_fusion.3 = (f32[1,8,256,256]{3,2,1,0:T(8,128)S(1)}, f32[1,8,256,256]{3,2,1,0:T(8,128)S(1)}) fusion(f32[8,256]{1,0:T(8,128)S(1)} %get-tuple-element.51, f32[8,256]{1,0:T(8,128)S(1)} %get-tuple-element.52, f32[8,256]{1,0:T(8,128)S(1)} %get-tuple-element.47, f32[8,256]{1,0:T(8,128)S(1)} %get-tuple-element.48, f32[8,256]{1,0:T(8,128)S(1)} %get-tuple-element.53, ...), kind=kLoop, calls=%fused_computation.121 | loop fusion | flops 15728640 | bytes 8454144 | tf_op jit(solution)/shard_map/add | solution.py:42
  141.4 2.4 pad_maximum_fusion.1
  143.8 40.4 %all-reduce.8.cloned.1.call-done = f32[2,8,256,256]{3,2,1,0:T(8,128)} async-done(((f32[2,8,256,256]{3,2,1,0:T(8,128)}), f32[2,8,256,256]{3,2,1,0:T(8,128)}) %all-reduce.8.cloned.1.call-update) | async-done | bytes 4194320 | tf_op jit(solution)/shard_map/psum | solution.py:89
  184.2 8.1 %multiply_reduce_fusion.1 = (f32[8,256]{1,0:T(8,128)S(1)}, f32[8,256]{1,0:T(8,128)S(1)}, f32[8,256]{1,0:T(8,128)S(1)}, f32[8,256]{1,0:T(8,128)S(1)}) fusion(f32[8,256]{1,0:T(8,128)S(1)} %get-tuple-element.53, f32[8,256]{1,0:T(8,128)S(1)} %get-tuple-element.50, f32[256,256]{1,0:T(8,128)S(1)} %compare_convert_fusion, f32[8,256]{1,0:T(8,128)S(1)} %get-tuple-element.37, ...), kind=kLoop, calls=%fused_computation.111 | loop fusion | flops 29351936 | bytes 10846208 | tf_op jit(solution)/shard_map/reduce_sum | solution.py:110
  192.5 4.0 %multiply_reduce_fusion.5 = (f32[8,256]{1,0:T(8,128)S(1)}, f32[8,256]{1,0:T(8,128)S(1)}) fusion(f32[2,8,256,256]{3,2,1,0:T(8,128)S(1)} %copy-done.5, f32[8,256]{1,0:T(8,128)S(1)} %get-tuple-element.53, f32[8,256]{1,0:T(8,128)S(1)} %get-tuple-element.50, f32[8,256]{1,0:T(8,128)S(1)} %get-tuple-element.49, f32[8,256]{1,0:T(8,128)S(1)} %get-tuple-element.46, ...), kind=kLoop, calls=%fused_computation.117 | loop fusion | flops 19918848 | bytes 8716288 | tf_op jit(solution)/shard_map/reduce_sum | solution.py:106
  196.7 34.7 %all-reduce = (f32[2,2,2,256]{3,2,0,1:T(2,128)S(1)}, f32[2,2,256]{2,1,0:T(2,128)S(1)}) all-reduce(f32[2,2,2,256]{3,2,0,1:T(2,128)S(1)} %convolution_bitcast_fusion.6, f32[2,2,256]{2,1,0:T(2,128)S(1)} %fusion.99), channel_id=1, replica_groups=mesh['row'=8,'col'=8,'dir'=2] {'col'}, use_global_device_ids=true, to_apply=%region_16.17 | all-reduce | flops 3072 | bytes 24576 | tf_op jit(solution)/shard_map/psum | solution.py:115
  231.4 15.4 %psum.78 = f32[2,2,2,256]{3,2,0,1:T(2,128)S(1)} all-reduce(f32[2,2,2,256]{3,2,0,1:T(2,128)S(1)} %get-tuple-element.20), channel_id=1, replica_groups=mesh['row'=8,'col'=8,'dir'=2] {'row'}, use_global_device_ids=true, to_apply=%region_20.21 | all-reduce | flops 2048 | bytes 16384 | tf_op jit(solution)/shard_map/psum | solution.py:11
  247.2 4.3 %add_add_fusion = (f32[1,8,256,256]{3,2,1,0:T(8,128)S(1)}, f32[1,8,256,256]{3,2,1,0:T(8,128)S(1)}) fusion(f32[8,256]{1,0:T(8,128)S(1)} %get-tuple-element.43, f32[8,256]{1,0:T(8,128)S(1)} %get-tuple-element.44, f32[8,256]{1,0:T(8,128)S(1)} %get-tuple-element.39, f32[8,256]{1,0:T(8,128)S(1)} %get-tuple-element.40, f32[8,256]{1,0:T(8,128)S(1)} %get-tuple-element.45, ...), kind=kLoop, calls=%fused_computation.109 | loop fusion | flops 15728640 | bytes 8454144 | tf_op jit(solution)/shard_map/add | solution.py:42
  251.6 2.4 pad_maximum_fusion.2
  254.0 0.6 copy.9
  254.6 39.8 %all-reduce.10.cloned.1.call-done = f32[2,8,256,256]{3,2,1,0:T(8,128)} async-done(((f32[2,8,256,256]{3,2,1,0:T(8,128)}), f32[2,8,256,256]{3,2,1,0:T(8,128)}) %all-reduce.10.cloned.1.call-update) | async-done | bytes 4194320 | tf_op jit(solution)/shard_map/psum | solution.py:89
  294.4 2.8 convert_subtract_fusion
  297.2 1.5 fusion.88
  (47 shorter events, 2.0 us)
Async XLA Ops:
  7.2 23.5 %copy-start = (s32[4,8]{1,0:T(4,128)S(1)}, s32[4,8]{1,0:T(4,128)}, u32[]{:S(2)}) copy-start(s32[4,8]{1,0:T(4,128)} %param.8) | copy-start | bytes 388
  7.2 66.8 %all-reduce.6.cloned.1.call-start = ((), (), s32[]{:S(2)}) async-start(), calls=%async_computation | async-start | bytes 8388608 | tf_op jit(solution)/shard_map/psum | solution.py:89
  38.6 0.8 copy-start.6
  38.6 35.4 %copy-start.3 = (bf16[2,8,256,256]{3,2,1,0:T(8,128)(2,1)S(1)}, bf16[2,8,256,256]{3,2,1,0:T(8,128)(2,1)}, u32[]{:S(2)}) copy-start(bf16[2,8,256,256]{3,2,1,0:T(8,128)(2,1)} %param.5) | copy-start | bytes 6291460
  38.6 145.6 %all-reduce.8.cloned.1.call-start = ((), (), s32[]{:S(2)}) async-start(), calls=%async_computation.1 | async-start | bytes 8388608 | tf_op jit(solution)/shard_map/psum | solution.py:89
  74.0 8.3 %copy-start.1 = (bf16[2,2,8,256,256]{4,3,2,1,0:T(8,128)(2,1)S(1)}, bf16[2,2,8,256,256]{4,3,2,1,0:T(8,128)(2,1)}, u32[]{:S(2)}) copy-start(bf16[2,2,8,256,256]{4,3,2,1,0:T(8,128)(2,1)} %param.6) | copy-start | bytes 12582916
  74.0 8.3 %copy-start.4 = (f32[2,8,256,256]{3,2,1,0:T(8,128)S(1)}, f32[2,8,256,256]{3,2,1,0:T(8,128)}, u32[]{:S(2)}) copy-start(f32[2,8,256,256]{3,2,1,0:T(8,128)} %all-reduce.6.cloned.1.call-done) | copy-start | bytes 12582916
  143.8 150.6 %all-reduce.10.cloned.1.call-start = ((), (), s32[]{:S(2)}) async-start(), calls=%async_computation.2 | async-start | bytes 8388608 | tf_op jit(solution)/shard_map/psum | solution.py:89
  184.2 8.3 %copy-start.2 = (bf16[2,2,8,256,256]{4,3,2,1,0:T(8,128)(2,1)S(1)}, bf16[2,2,8,256,256]{4,3,2,1,0:T(8,128)(2,1)}, u32[]{:S(2)}) copy-start(bf16[2,2,8,256,256]{4,3,2,1,0:T(8,128)(2,1)} %param.6) | copy-start | bytes 12582916
  184.2 8.3 %copy-start.5 = (f32[2,8,256,256]{3,2,1,0:T(8,128)S(1)}, f32[2,8,256,256]{3,2,1,0:T(8,128)}, u32[]{:S(2)}) copy-start(f32[2,8,256,256]{3,2,1,0:T(8,128)} %all-reduce.8.cloned.1.call-done) | copy-start | bytes 12582916
Sparse Core Ops, SparseCore 0:
  38.7 35.2 all-reduce.5
  143.9 40.2 all-reduce.7
  254.1 40.2 all-reduce.9
where the time goes:
time: 306 us; the launch traced here: 305 us
  blocking collectives  123 us (40%)
  waiting for transfers between devices  115 us (38%)
  other arithmetic  49.6 us (16%)
  between operations  14 us (5%)
    psum x3, waiting for transfers between devices, residual_of(): partial_value = lax.psum(partial_value, 'dir')  115 us
    psum x2, blocking collectives, body(): numer_rows, denom_rows = lax.psum((numer_rows, denom_rows), 'col')  69.5 us
    psum x3, blocking collectives, from_root(): return lax.psum(kept, axis)  53.5 us
    reduce_sum x2, other arithmetic, body(): jnp.sum(weight * (pair_re * pair_re + pair_im * pair_im), axis=2)  16.3 us
    add x3, other arithmetic, sum_terms(): total = total + entry  13 us
    reduce_sum x2, other arithmetic, body(): jnp.sum(weight * (data_re * pair_re + data_im * pair_im), axis=2)  8.01 us
    another operation x3, other arithmetic, residual_of(): jnp.stack([sum_terms([entry[0] for entry in preds]), sum_terms([entry[1]...  7.19 us
  transfers between devices with their start and end apart: 3, of which 3 were waited for; matrix products, arithmetic and copies ran while one was open for 0% of the time, Pallas kernels for 0%

commit v1 on v0

v1 whole, which is shorter than its diff:
```python
import functools

import jax
import jax.numpy as jnp
from jax import lax
from jax.experimental import pallas as pl
from jax.experimental.pallas import tpu as pltpu
from jax.sharding import PartitionSpec as P

ITERS = 2
MESH = pl.DeviceIdType.MESH
F32, BF16 = jnp.float32, jnp.bfloat16
TILE = 16


def rows_like(shape):
    return lax.broadcasted_iota(jnp.int32, shape, 0)


def turned(g):
    count = g.shape[0] // 8
    out = []
    for k in range(count):
        out += [-g[8 * k + 4 : 8 * k + 8], g[8 * k : 8 * k + 4]]
    return jnp.concatenate(out, axis=0)


def halves(x):
    high = x.astype(BF16)
    return high, (x - high.astype(F32)).astype(BF16)


def outer_products(a_ref, g_rows, g_cols):
    width = g_cols.shape[1]
    right = jnp.concatenate([g_cols, turned(g_cols)], axis=1)
    right_hi, right_lo = halves(right)
    right_all = jnp.concatenate([right_hi, right_lo, right_hi], axis=0)
    left_hi, left_lo = halves(g_rows)
    row = rows_like((48, g_rows.shape[1]))
    left_all = jnp.concatenate([left_hi, left_hi, left_lo], axis=0).astype(F32)
    for k in range(2):
        for d in range(4):
            at = row % 16
            keep = (at == 8 * k + d) | (at == 8 * k + 4 + d)
            left = jnp.where(keep, left_all, 0.0).astype(BF16)
            a_ref[k * 4 + d] = lax.dot_general(
                left, right_all, (((0,), (0,)), ((), ())), preferred_element_type=F32
            )


def channel_rows(g, picks):
    at = rows_like((8, g.shape[1])) % 4
    second = jnp.zeros(at.shape, jnp.int32)
    for d in range(4):
        second = jnp.where(at == d, picks[d], second)
    return jnp.where(second == 1, g[8:16], g[0:8]), second


def kernel(
    n_row, n_col,
    vis, model, gains, mask, idx,
    gains_out, res_out,
    m_v, v_v, mf_v, vf_v, d_v, a_v, a2_v, t_v, off_v, fr_v, fc_v, fri_v, fci_v, out_v,
    gin_c, gin_r, g_r, g_c, g_r2, colb, rowb,
    loc_sem, out_sem, mod_s, mod_r, gs_s, gs_r, gr_s, gr_r, col_s, col_r, row_s, row_r, fin_s, fin_r,
):
    r, c, e = lax.axis_index("row"), lax.axis_index("col"), lax.axis_index("dir")
    other = 1 - e
    sib = (r, c, other)
    half = model.shape[3] // 2
    chans = model.shape[2]
    fin = chans // 2

    def row_peer(k, x):
        return lax.rem(r + k, n_row), c, lax.rem(e + x, 2)

    def col_peer(k, x):
        return r, lax.rem(c + k, n_col), lax.rem(e + x, 2)

    row_list = [(k, x) for k in range(n_row) for x in range(2) if (k, x) != (0, 0)]
    col_list = [(k, x) for k in range(1, n_col) for x in range(2)]

    barrier = pltpu.get_barrier_semaphore()
    for k, x in col_list:
        pl.semaphore_signal(barrier, inc=1, device_id=col_peer(k, x), device_id_type=MESH)
    for k, x in row_list:
        pl.semaphore_signal(barrier, inc=1, device_id=row_peer(k, x), device_id_type=MESH)

    mine = pl.ds(pl.multiple_of(e * half, half), half)
    theirs = pl.ds(pl.multiple_of(other * half, half), half)
    my_ch = pl.ds(e * fin, fin)
    their_ch = pl.ds(other * fin, fin)
    block_r = pl.ds(pl.multiple_of(r * 2 * half + e * half, half), half)
    block_c = pl.ds(pl.multiple_of(c * 2 * half, 2 * half), 2 * half)
    local = [
        (gains, gin_c.at[e]),
        (mask.at[:, block_r], fri_v),
        (mask.at[:, block_c], fci_v),
        (vis.at[:, :, mine, :], v_v),
        (vis.at[:, my_ch, theirs, :], vf_v),
        (model.at[:, :, :, mine, :], m_v.at[pl.ds(2 * e, 2)]),
        (model.at[:, :, my_ch, theirs, :], mf_v.at[pl.ds(2 * e, 2)]),
    ]
    local = [pltpu.make_async_copy(s, d, loc_sem.at[i]) for i, (s, d) in enumerate(local)]
    for cp in local:
        cp.start()

    def remote(src, dst, send, recv, device):
        return pltpu.make_async_remote_copy(
            src_ref=src, dst_ref=dst, send_sem=send, recv_sem=recv,
            device_id=device, device_id_type=MESH,
        )

    local[0].wait()
    pl.semaphore_wait(barrier, len(col_list) + len(row_list))

    gains_sib = remote(gin_c.at[e], gin_c.at[e], gs_s, gs_r, sib)
    diag = r == c

    @pl.when(diag)
    def _():
        for i, (k, x) in enumerate(col_list):
            remote(gin_c.at[e], gin_r.at[e], gr_s.at[i], gr_r.at[e], col_peer(k, x)).start()

    gains_sib.start()
    model_a = remote(
        model.at[:, :, :, theirs, :], m_v.at[pl.ds(2 * e, 2)], mod_s.at[0], mod_r.at[0], sib
    )
    model_b = remote(
        model.at[:, :, their_ch, mine, :], mf_v.at[pl.ds(2 * e, 2)], mod_s.at[1], mod_r.at[1], sib
    )
    model_a.start()
    model_b.start()

    for cp in local[1:]:
        cp.wait()
    fr_v[...] = fri_v[...].astype(F32)
    fc_v[...] = fci_v[...].astype(F32)
    p_at = r * 2 * half + e * half + rows_like(off_v.shape)
    q_at = c * 2 * half + lax.broadcasted_iota(jnp.int32, off_v.shape, 1)
    off_v[...] = jnp.where(p_at == q_at, 0.0, 1.0).astype(BF16)

    gains_sib.wait_recv()
    for s in range(2):
        for x in range(2):
            for l in range(2):
                for k in range(2):
                    at = k * 8 + x * 4 + s * 2 + l
                    g_c[at : at + 1, :] = gin_c[s, x, l, k : k + 1, :]

    model_a.wait_recv()

    def squares(ch, _):
        for d in range(4):
            for t in range(half // TILE):
                rows = slice(t * TILE, (t + 1) * TILE)
                re = m_v[d, 0, ch, rows, :].astype(F32)
                im = m_v[d, 1, ch, rows, :].astype(F32)
                sq = (re * re + im * im).astype(BF16) * off_v[rows, :]
                at = (d % 2) * half + t * TILE
                d_v[ch, d // 2, at : at + TILE, :] = sq
        return 0

    lax.fori_loop(0, chans, squares, 0)

    @pl.when(diag)
    def _():
        gin_r[...] = gin_c[...]

    @pl.when(jnp.logical_not(diag))
    def _():
        for s in range(2):
            remote(gin_c.at[s], gin_r.at[s], gr_s.at[0], gr_r.at[s], sib).wait_recv()

    lanes = pl.ds(pl.multiple_of(e * half, half), half)
    for s in range(2):
        for x in range(2):
            for l in range(2):
                for k in range(2):
                    at = k * 8 + x * 4 + s * 2 + l
                    g_r[at : at + 1, :] = gin_r[s, x, l, k : k + 1, lanes]

    def residual_tile(a, mod, vi, ch, picks, rows):
        re = vi[0, ch, rows, :].astype(F32)
        im = vi[1, ch, rows, :].astype(F32)
        width = re.shape[1]
        for d in range(4):
            at = picks[d] * 4 + d
            a_re = a[at, rows, 0:width]
            a_im = a[at, rows, width : 2 * width]
            m_re = mod[d, 0, ch, rows, :].astype(F32)
            m_im = mod[d, 1, ch, rows, :].astype(F32)
            re = re - a_re * m_re + a_im * m_im
            im = im - a_re * m_im - a_im * m_re
        return re, im

    def sweep(step):
        gr, gc = g_r[...], g_c[...]
        outer_products(a_v, gr, gc)
        zeros_c = jnp.zeros((24, gc.shape[1]), F32)
        zeros_r = jnp.zeros((24, gr.shape[1]), F32)

        def channel(ch, carry):
            col, row = carry
            picks = [idx[d, ch] for d in range(4)]
            for t in range(half // TILE):
                rows = slice(t * TILE, (t + 1) * TILE)
                re, im = residual_tile(a_v, m_v, v_v, ch, picks, rows)
                re = re.astype(BF16) * off_v[rows, :]
                im = im.astype(BF16) * off_v[rows, :]
                for d in range(4):
                    m_re = m_v[d, 0, ch, rows, :]
                    m_im = m_v[d, 1, ch, rows, :]
                    t_v[d, t * TILE : (t + 1) * TILE, :] = re * m_re + im * m_im
                    at = half + t * TILE
                    t_v[d, at : at + TILE, :] = re * m_im - im * m_re
            f_r = fr_v[pl.ds(ch, 1), :]
            f_c = fc_v[pl.ds(ch, 1), :]
            x_r, second_r = channel_rows(gr, picks)
            x_c, second_c = channel_rows(gc, picks)
            x_r = x_r * f_r
            x_c = x_c * f_c
            x_col = jnp.concatenate([x_r, turned(x_r)], axis=1).astype(BF16)
            x_row = x_c.astype(BF16)
            at_c = rows_like(x_c.shape) % 4
            o_col = jnp.zeros(x_c.shape, F32)
            o_row = jnp.zeros(x_c.shape, F32)
            for d in range(4):
                got = jnp.dot(x_col, t_v[d], preferred_element_type=F32)
                o_col = jnp.where(at_c == d, got, o_col)
                got = lax.dot_general(
                    x_row, t_v[d], (((1,), (1,)), ((), ())), preferred_element_type=F32
                )
                o_row = jnp.where(at_c == d, got, o_row)
            back = -turned(o_row[:, half:])
            o_row = o_row[:, :half] + back
            s_r = x_r[0:4] * x_r[0:4] + x_r[4:8] * x_r[4:8]
            s_c = x_c[0:4] * x_c[0:4] + x_c[4:8] * x_c[4:8]
            at_4 = rows_like(s_r.shape)
            at_4c = rows_like(s_c.shape)
            den_c = jnp.zeros(s_c.shape, F32)
            den_r = jnp.zeros(s_r.shape, F32)
            for pair in range(2):
                left = jnp.concatenate(
                    [jnp.where(at_4 == 2 * pair + i, s_r, 0.0) for i in range(2)], axis=1
                ).astype(BF16)
                den_c += jnp.dot(left, d_v[ch, pair], preferred_element_type=F32)
                got = lax.dot_general(
                    s_c.astype(BF16), d_v[ch, pair], (((1,), (1,)), ((), ())),
                    preferred_element_type=F32,
                )
                for i in range(2):
                    den_r = jnp.where(at_4 == 2 * pair + i, got[:, i * half : (i + 1) * half], den_r)
            col_new = jnp.concatenate([o_col, den_c], axis=0) * f_c
            row_new = jnp.concatenate([o_row, den_r], axis=0) * f_r
            pick_c = jnp.concatenate([second_c, second_c[0:4]], axis=0) == 1
            pick_r = jnp.concatenate([second_r, second_r[0:4]], axis=0) == 1
            col = col + jnp.concatenate(
                [jnp.where(pick_c, 0.0, col_new), jnp.where(pick_c, col_new, 0.0)], axis=0
            )
            row = row + jnp.concatenate(
                [jnp.where(pick_r, 0.0, row_new), jnp.where(pick_r, row_new, 0.0)], axis=0
            )
            return col, row

        col, row = lax.fori_loop(0, chans, channel, (zeros_c, zeros_r))
        colb[step, r * 2 + e] = col
        rowb[step, c] = row
        col_copies, row_copies = [], []
        own = r * 2 + e
        for i in range(1, n_col):
            cp = remote(
                rowb.at[step, c], rowb.at[step, c], row_s.at[step, i], row_r.at[step, c],
                col_peer(i, 0),
            )
            cp.start()
            row_copies.append(cp)
        for i, (k, x) in enumerate(row_list):
            cp = remote(
                colb.at[step, own], colb.at[step, own], col_s.at[step, i], col_r.at[step, own],
                row_peer(k, x),
            )
            cp.start()
            col_copies.append(cp)
        for i in range(1, n_col):
            src = lax.rem(c + i, n_col)
            remote(
                rowb.at[step, src], rowb.at[step, src], row_s.at[step, i], row_r.at[step, src],
                col_peer(i, 0),
            ).wait_recv()
        for i, (k, x) in enumerate(row_list):
            src = lax.rem(r + k, n_row) * 2 + lax.rem(e + x, 2)
            remote(
                colb.at[step, src], colb.at[step, src], col_s.at[step, i], col_r.at[step, src],
                row_peer(k, x),
            ).wait_recv()

        def refresh(g, total):
            out = []
            for k in range(2):
                den = total[12 * k + 8 : 12 * k + 12] + 1.0
                den = jnp.concatenate([den, den], axis=0)
                out.append(g[8 * k : 8 * k + 8] + 0.5 * total[12 * k : 12 * k + 8] / den)
            return jnp.concatenate(out, axis=0)

        total = rowb[step, 0]
        for i in range(1, n_col):
            total = total + rowb[step, i]
        g_r[...] = refresh(gr, total)
        total = colb[step, 0]
        for i in range(1, 2 * n_row):
            total = total + colb[step, i]
        g_c[...] = refresh(gc, total)
        return col_copies + row_copies

    copies = []
    for step in range(ITERS):
        copies += sweep(step)

    g_r2[e] = g_r[...]
    rows_sib = remote(g_r2.at[e], g_r2.at[e], fin_s, fin_r, sib)
    rows_sib.start()

    for x in range(2):
        for l in range(2):
            for k in range(2):
                at = k * 8 + x * 4 + l
                gains_out[x, l, k : k + 1, :] = jnp.where(
                    e == 0, g_c[at : at + 1, :], g_c[at + 2 : at + 3, :]
                )

    def finish(a, mod, vi, where, base, which):
        def channel(ch, _):
            picks = [idx[d, e * fin + ch] for d in range(4)]
            for t in range(half // TILE):
                rows = slice(t * TILE, (t + 1) * TILE)
                re, im = residual_tile(a, mod, vi, base + ch, picks, rows)
                out_v[which, 0, ch, rows, :] = re
                out_v[which, 1, ch, rows, :] = im
            pltpu.make_async_copy(
                out_v.at[which, :, ch], res_out.at[:, ch, where, :], out_sem.at[which, ch]
            ).start()
            return 0

        lax.fori_loop(0, fin, channel, 0)

    outer_products(a_v, g_r[...], g_c[...])
    finish(a_v, m_v, v_v, mine, e * fin, 0)
    rows_back = remote(g_r2.at[other], g_r2.at[other], fin_s, fin_r, sib)
    rows_back.wait_recv()
    outer_products(a2_v, g_r2[other], g_c[...])
    model_b.wait_recv()
    finish(a2_v, mf_v, vf_v, theirs, 0, 1)

    model_a.wait_send()
    model_b.wait_send()
    gains_sib.wait_send()

    @pl.when(diag)
    def _():
        for i, (k, x) in enumerate(col_list):
            remote(gin_c.at[e], gin_r.at[e], gr_s.at[i], gr_r.at[e], col_peer(k, x)).wait_send()

    for cp in copies:
        cp.wait_send()
    rows_sib.wait_send()
    for which, where in enumerate((mine, theirs)):
        for ch in range(fin):
            pltpu.make_async_copy(
                out_v.at[which, :, ch], res_out.at[:, ch, where, :], out_sem.at[which, ch]
            ).wait()


def body(n_row, n_col, vis, model, gains, channel_interval_index, antenna_usable_mask):
    dirs, _, chans, rows, cols = model.shape
    half = rows // 2
    fin = chans // 2
    n_dir = 2 * dirs
    any_space = pl.BlockSpec(memory_space=pl.ANY)
    dma = pltpu.SemaphoreType.DMA
    return pl.pallas_call(
        functools.partial(kernel, n_row, n_col),
        out_shape=(
            jax.ShapeDtypeStruct(gains.shape, F32),
            jax.ShapeDtypeStruct((2, fin, rows, cols), F32),
        ),
        in_specs=[any_space] * 4 + [pl.BlockSpec(memory_space=pltpu.SMEM)],
        out_specs=(pl.BlockSpec(memory_space=pltpu.VMEM), any_space),
        scratch_shapes=[
            pltpu.VMEM((n_dir, 2, chans, half, cols), BF16),
            pltpu.VMEM((2, chans, half, cols), BF16),
            pltpu.VMEM((n_dir, 2, fin, half, cols), BF16),
            pltpu.VMEM((2, fin, half, cols), BF16),
            pltpu.VMEM((chans, 2, 2 * half, cols), BF16),
            pltpu.VMEM((8, half, 2 * cols), F32),
            pltpu.VMEM((8, half, 2 * cols), F32),
            pltpu.VMEM((n_dir, 2 * half, cols), BF16),
            pltpu.VMEM((half, cols), BF16),
            pltpu.VMEM((chans, half), F32),
            pltpu.VMEM((chans, cols), F32),
            pltpu.VMEM((chans, half), jnp.int32),
            pltpu.VMEM((chans, cols), jnp.int32),
            pltpu.VMEM((2, 2, fin, half, cols), F32),
            pltpu.VMEM((2,) + gains.shape, F32),
            pltpu.VMEM((2,) + gains.shape, F32),
            pltpu.VMEM((16, half), F32),
            pltpu.VMEM((16, cols), F32),
            pltpu.VMEM((2, 16, half), F32),
            pltpu.VMEM((ITERS, 2 * n_row, 24, cols), F32),
            pltpu.VMEM((ITERS, n_col, 24, half), F32),
            dma((7,)),
            dma((2, fin)),
            dma((2,)),
            dma((2,)),
            dma,
            dma,
            dma((2 * n_col,)),
            dma((2,)),
            dma((ITERS, 2 * n_row)),
            dma((ITERS, 2 * n_row)),
            dma((ITERS, n_col)),
            dma((ITERS, n_col)),
            dma,
            dma,
        ],
        compiler_params=pltpu.CompilerParams(
            collective_id=0, has_side_effects=True, vmem_limit_bytes=48 * 2**20
        ),
    )(vis, model, gains, antenna_usable_mask, channel_interval_index)


def solution(mesh):
    placed = (
        P(None, None, "row", "col"),
        P("dir", None, None, "row", "col"),
        P(None, "dir", None, "col"),
        P(),
        P(),
    )
    return jax.shard_map(
        functools.partial(body, mesh.shape["row"], mesh.shape["col"]),
        mesh=mesh,
        in_specs=placed,
        out_specs=(P(None, "dir", None, "col"), P(None, "dir", "row", "col")),
        check_vma=False,
    )
```

time: 306 us -> 50.7 us (0.17)
  blocking collectives: 123 us -> 0 us
  waiting for transfers between devices: 115 us -> 0 us
  other arithmetic: 49.6 us -> 0 us
  Pallas kernels: 0 us -> 44.1 us
  between operations: 14 us -> 0.65 us
  local copies, waits for them, and re-layouts: 1.45 us -> 5.72 us
    psum x5 -> x0, blocking collectives: 123 us -> none  [the longest x2 69.5 us: body(): numer_rows, denom_rows = lax.psum((numer_rows, denom_rows), 'col')]
    psum x3 -> x0, waiting for transfers between devices: 115 us -> none  [residual_of(): partial_value = lax.psum(partial_value, 'dir')]
    pallas_call x0 -> x1, Pallas kernels: none -> 44.1 us  [body(): pl.pallas_call(functools.partial(kernel, n_row, n_col), out_shape=(jax.Sh...]
    reduce_sum x4 -> x0, other arithmetic: 24.3 us -> none  [the longest x2 16.3 us: body(): jnp.sum(weight * (pair_re * pair_re + pair_im * pair_im), axis=2)]
    add x6 -> x0, other arithmetic: 13 us -> none  [the longest x3 13 us: sum_terms(): total = total + entry]
    another operation x8 -> x0, other arithmetic: 8.67 us -> none  [the longest x3 7.19 us: residual_of(): jnp.stack([sum_terms([entry[0] for entry in preds]), sum_terms([entry[1]...]
    unnamed x15 -> x10, local copies, waits for them, and re-layouts: 1.39 us -> 5.72 us
  transfers between devices with their start and end apart: 3 -> 0, of which waited for: 3 -> 0; matrix products, arithmetic and copies ran while one was open for 0% -> 0% of each run, Pallas kernels for 0% -> 0%
where the time goes in v1:
time: 50.7 us; the launch traced here: 50.5 us
  Pallas kernels  44.1 us (87%)
  local copies, waits for them, and re-layouts  5.72 us (11%)
  between operations  0.65 us (1%)
    pallas_call x1, Pallas kernels, body(): pl.pallas_call(functools.partial(kernel, n_row, n_col), out_shape=(jax.Sh...  44.1 us
    unnamed x10, local copies, waits for them, and re-layouts  5.72 us

profile of v1, /device:TPU:1, one launch (start us, length us, event | category | flops | bytes accessed | tf_op | source)
XLA Modules:
  0.0 50.5 jit_solution(17384578899599670404)
XLA Ops:
  0.6 0.0 copy-start
  0.6 1.6 %copy-done = bf16[2,8,256,256]{3,2,1,0:T(8,128)(2,1)S(1)} copy-done((bf16[2,8,256,256]{3,2,1,0:T(8,128)(2,1)S(1)}, bf16[2,8,256,256]{3,2,1,0:T(8,128)(2,1)}, u32[]{:S(2)}) %copy-start) | copy-done | bytes 2097176
  2.2 0.0 copy-start.1
  2.2 0.8 %copy-done.1 = s32[8,2048]{1,0:T(8,128)S(1)} copy-done((s32[8,2048]{1,0:T(8,128)S(1)}, s32[8,2048]{1,0:T(8,128)}, u32[]{:S(2)}) %copy-start.1) | copy-done | bytes 65560
  3.1 0.0 copy-start.2
  3.1 0.7 %copy-done.2 = f32[2,2,2,256]{3,2,1,0:T(2,128)S(1)} copy-done((f32[2,2,2,256]{3,2,1,0:T(2,128)S(1)}, f32[2,2,2,256]{3,2,1,0:T(2,128)}, u32[]{:S(2)}) %copy-start.2) | copy-done | bytes 8216
  3.8 0.0 copy-start.3
  3.8 0.7 %copy-done.3 = s32[4,8]{1,0:T(4,128)S(1)} copy-done((s32[4,8]{1,0:T(4,128)S(1)}, s32[4,8]{1,0:T(4,128)}, u32[]{:S(2)}) %copy-start.3) | copy-done | bytes 152
  4.4 44.1 %shard_map.68 = (f32[2,2,2,256]{3,2,1,0:T(2,128)S(1)}, f32[2,4,256,256]{3,2,1,0:T(8,128)S(1)}) custom-call(bf16[2,8,256,256]{3,2,1,0:T(8,128)(2,1)S(1)} %copy-done, bf16[2,2,8,256,256]{4,3,2,1,0:T(8,128)(2,1)} %model.1, f32[2,2,2,256]{3,2,1,0:T(2,128)S(1)} %copy-done.2, s32[8,2048]{1,0:T(8,128)S(1)} %copy-done.1, s32[4,8]{1,0:T(4,128)S(1)} %copy-done.3), custom_call_target="tpu_custom_call" | custom-call | tf_op jit(solution)/shard_map/pallas_call | solution.py:381
  48.5 0.6 %copy.9 = f32[2,2,2,256]{3,2,1,0:T(2,128)} copy(f32[2,2,2,256]{3,2,1,0:T(2,128)S(1)} %get-tuple-element.4) | data formatting | bytes 16384
  49.1 1.3 %copy.10 = f32[2,4,256,256]{3,2,1,0:T(8,128)} copy(f32[2,4,256,256]{3,2,1,0:T(8,128)S(1)} %get-tuple-element.5) | data formatting | bytes 4194304
Async XLA Ops:
  0.6 1.6 %copy-start = (bf16[2,8,256,256]{3,2,1,0:T(8,128)(2,1)S(1)}, bf16[2,8,256,256]{3,2,1,0:T(8,128)(2,1)}, u32[]{:S(2)}) copy-start(bf16[2,8,256,256]{3,2,1,0:T(8,128)(2,1)} %vis.1) | copy-start | bytes 6291460
  2.2 0.8 %copy-start.1 = (s32[8,2048]{1,0:T(8,128)S(1)}, s32[8,2048]{1,0:T(8,128)}, u32[]{:S(2)}) copy-start(s32[8,2048]{1,0:T(8,128)} %mask.1) | copy-start | bytes 196612
  3.1 0.7 %copy-start.2 = (f32[2,2,2,256]{3,2,1,0:T(2,128)S(1)}, f32[2,2,2,256]{3,2,1,0:T(2,128)}, u32[]{:S(2)}) copy-start(f32[2,2,2,256]{3,2,1,0:T(2,128)} %gains.1) | copy-start | bytes 24580
  3.8 0.7 %copy-start.3 = (s32[4,8]{1,0:T(4,128)S(1)}, s32[4,8]{1,0:T(4,128)}, u32[]{:S(2)}) copy-start(s32[4,8]{1,0:T(4,128)} %idx.1) | copy-start | bytes 388

commit v2 on v1

v2 whole, which is shorter than its diff:
```python
import functools

import jax
import jax.numpy as jnp
from jax import lax
from jax.experimental import pallas as pl
from jax.experimental.pallas import tpu as pltpu
from jax.sharding import PartitionSpec as P

ITERS = 2
MESH = pl.DeviceIdType.MESH
F32, BF16 = jnp.float32, jnp.bfloat16
TILE = 16


def rows_like(shape):
    return lax.broadcasted_iota(jnp.int32, shape, 0)


def turned(g):
    count = g.shape[0] // 8
    out = []
    for k in range(count):
        out += [-g[8 * k + 4 : 8 * k + 8], g[8 * k : 8 * k + 4]]
    return jnp.concatenate(out, axis=0)


def halves(x):
    high = x.astype(BF16)
    return high, (x - high.astype(F32)).astype(BF16)


def outer_products(a_ref, g_rows, g_cols):
    width = g_cols.shape[1]
    right = jnp.concatenate([g_cols, turned(g_cols)], axis=1)
    right_hi, right_lo = halves(right)
    right_all = jnp.concatenate([right_hi, right_lo, right_hi], axis=0)
    left_hi, left_lo = halves(g_rows)
    row = rows_like((48, g_rows.shape[1]))
    left_all = jnp.concatenate([left_hi, left_hi, left_lo], axis=0).astype(F32)
    for k in range(2):
        for d in range(4):
            at = row % 16
            keep = (at == 8 * k + d) | (at == 8 * k + 4 + d)
            left = jnp.where(keep, left_all, 0.0).astype(BF16)
            a_ref[k * 4 + d] = lax.dot_general(
                left, right_all, (((0,), (0,)), ((), ())), preferred_element_type=F32
            )


def residual_tile(a, mod, vi, ch, picks, rows):
    re = vi[0, ch, rows, :].astype(F32)
    im = vi[1, ch, rows, :].astype(F32)
    width = re.shape[1]
    for d in range(4):
        at = picks[d] * 4 + d
        a_re = a[at, rows, 0:width]
        a_im = a[at, rows, width : 2 * width]
        m_re = mod[d, 0, ch, rows, :].astype(F32)
        m_im = mod[d, 1, ch, rows, :].astype(F32)
        re = re - a_re * m_re + a_im * m_im
        im = im - a_re * m_im - a_im * m_re
    return re, im


def kernel(
    n_row, n_col,
    vis, model, gains, mask, index,
    m_v, v_v, mf_v, vf_v, g_r2, g_c, idx,
    w_v, d_v, a_v, t_v, fri_v, fci_v, prev, last,
    gin_c, gin_r, g_r, colb, rowb, colt,
    loc_sem, mod_s, mod_r, gs_s, gs_r, gr_s, gr_r,
    col_s, col_r, row_s, row_r, ct_s, ct_r, fin_s, fin_r,
):
    r, c, e = lax.axis_index("row"), lax.axis_index("col"), lax.axis_index("dir")
    other = 1 - e
    sib = (r, c, other)
    half = model.shape[3] // 2
    chans = model.shape[2]
    fin = chans // 2
    quad = n_col // 2

    def row_peer(k):
        return lax.rem(r + k, n_row), c, e

    def col_peer(k):
        return r, lax.rem(c + k, n_col), e

    row_list = sorted(range(1, n_row), key=lambda k: (k % 2 == 0, abs(k - n_row // 2)))
    col_list = sorted(range(1, n_col), key=lambda k: abs(k - n_col // 2))

    flip_r = r + 1 - 2 * lax.rem(r, 2)
    flip_c = c + 1 - 2 * lax.rem(c, 2)
    near = r == c
    cross = r == flip_c
    same = lax.div(r, quad) == lax.div(c, quad)
    source_row = jnp.where(same, r, flip_r)
    near_to = [
        (r, lax.div(c, quad) * quad + lax.rem(c + k, quad), x)
        for k in range(1, quad) for x in range(2)
    ]
    cross_to = [
        (c, (1 - lax.div(c, quad)) * quad + k, x) for k in range(quad) for x in range(2)
    ]

    barrier = pltpu.get_barrier_semaphore()

    @pl.when(jnp.logical_not(near))
    def _():
        for x in range(2):
            pl.semaphore_signal(
                barrier, inc=1, device_id=(source_row, r, x), device_id_type=MESH
            )

    for k in col_list:
        pl.semaphore_signal(barrier, inc=1, device_id=col_peer(k), device_id_type=MESH)
    for k in row_list:
        pl.semaphore_signal(barrier, inc=1, device_id=row_peer(k), device_id_type=MESH)
    pl.semaphore_signal(barrier, inc=1, device_id=sib, device_id_type=MESH)

    mine = pl.ds(pl.multiple_of(e * half, half), half)
    theirs = pl.ds(pl.multiple_of(other * half, half), half)
    my_ch = pl.ds(e * fin, fin)
    their_ch = pl.ds(other * fin, fin)
    block_r = pl.ds(pl.multiple_of(r * 2 * half + e * half, half), half)
    block_c = pl.ds(pl.multiple_of(c * 2 * half, 2 * half), 2 * half)
    own_dirs = pl.ds(2 * e, 2)
    local = [
        (gains, gin_c.at[e]),
        (index, idx),
        (mask.at[:, block_r], fri_v),
        (mask.at[:, block_c], fci_v),
        (model.at[:, :, :, mine, :], m_v.at[own_dirs]),
        (vis.at[:, :, mine, :], v_v),
        (vis.at[:, my_ch, theirs, :], vf_v),
        (model.at[:, :, my_ch, theirs, :], mf_v.at[own_dirs]),
    ]
    local = [pltpu.make_async_copy(s, d, loc_sem.at[i]) for i, (s, d) in enumerate(local)]
    for cp in local:
        cp.start()

    def remote(src, dst, send, recv, device):
        return pltpu.make_async_remote_copy(
            src_ref=src, dst_ref=dst, send_sem=send, recv_sem=recv,
            device_id=device, device_id_type=MESH,
        )

    local[0].wait()
    n_near, n_cross = len(near_to), len(cross_to)
    pl.semaphore_wait(
        barrier,
        len(col_list) + len(row_list) + 1
        + jnp.where(near, n_near, 0) + jnp.where(cross, n_cross, 0),
    )

    def gains_to(devices):
        return [
            remote(gin_c.at[e], gin_r.at[e], gr_s.at[i], gr_r.at[e], to)
            for i, to in enumerate(devices)
        ]

    @pl.when(near)
    def _():
        for cp in gains_to(near_to):
            cp.start()

    @pl.when(cross)
    def _():
        for cp in gains_to(cross_to):
            cp.start()

    gains_sib = remote(gin_c.at[e], gin_c.at[e], gs_s, gs_r, sib)
    gains_sib.start()
    model_a = [
        remote(
            model.at[l, :, :, theirs, :], m_v.at[2 * e + l], mod_s.at[l], mod_r.at[l], sib
        )
        for l in range(2)
    ]
    model_b = remote(
        model.at[:, :, their_ch, mine, :], mf_v.at[own_dirs], mod_s.at[2], mod_r.at[2], sib
    )
    for cp in model_a:
        cp.start()
    model_b.start()

    for cp in local[1:4]:
        cp.wait()
    for d in range(4):
        ends = [jnp.int32(chans), jnp.int32(chans)]
        for ch in range(chans):
            second = idx[d, ch] == 1
            prev[d, ch] = jnp.where(second, ends[1], ends[0])
            ends = [jnp.where(second, ends[0], ch), jnp.where(second, ch, ends[1])]
        for k in range(2):
            last[k, d] = ends[k]
    t_v[chans] = jnp.zeros(t_v.shape[1:], BF16)
    shape = (half, 2 * half)
    p_at = r * 2 * half + e * half + rows_like(shape)
    q_at = c * 2 * half + lax.broadcasted_iota(jnp.int32, shape, 1)
    apart = p_at != q_at
    f_r = fri_v[...].astype(F32)
    f_c = fci_v[...].astype(F32).astype(BF16)
    for ch in range(chans):
        one = jnp.where(rows_like(f_r.shape) == ch, f_r, 0.0).astype(BF16)
        both = lax.dot_general(
            one, f_c, (((0,), (0,)), ((), ())), preferred_element_type=F32
        )
        w_v[ch] = jnp.where(apart, both, 0.0).astype(BF16)

    def squares(core, l):
        d = 2 * core + l

        def tile(t, _):
            at = pl.multiple_of(t * TILE, TILE)
            rows = pl.ds(at, TILE)
            total = [jnp.zeros((TILE, 2 * half), F32)] * 2
            for ch in range(chans):
                re = m_v[d, 0, ch, rows, :].astype(F32)
                im = m_v[d, 1, ch, rows, :].astype(F32)
                sq = (re * re + im * im) * w_v[ch, rows, :].astype(F32)
                second = idx[d, ch].astype(F32)
                part = sq * second
                total = [total[0] + sq, total[1] + part]
            out = pl.ds(pl.multiple_of(l * half + at, TILE), TILE)
            d_v[core, out, :] = (total[0] - total[1]).astype(BF16)
            d_v[2 + core, out, :] = total[1].astype(BF16)
            return 0

        lax.fori_loop(0, half // TILE, tile, 0)

    local[4].wait()
    for l in range(2):
        squares(e, l)

    gains_sib.wait_recv()
    for s in range(2):
        for x in range(2):
            for l in range(2):
                for k in range(2):
                    at = k * 8 + x * 4 + s * 2 + l
                    g_c[at : at + 1, :] = gin_c[s, x, l, k : k + 1, :]

    for l in range(2):
        remote(
            model.at[l, :, :, theirs, :], m_v.at[2 * other + l], mod_s.at[l], mod_r.at[l], sib
        ).wait_recv()
        squares(other, l)

    @pl.when(near)
    def _():
        gin_r[...] = gin_c[...]

    @pl.when(jnp.logical_not(near))
    def _():
        for s in range(2):
            remote(gin_c.at[s], gin_r.at[s], gr_s.at[0], gr_r.at[s], sib).wait_recv()

    lanes = pl.ds(pl.multiple_of(e * half, half), half)
    for s in range(2):
        for x in range(2):
            for l in range(2):
                for k in range(2):
                    at = k * 8 + x * 4 + s * 2 + l
                    g_r[at : at + 1, :] = gin_r[s, x, l, k : k + 1, lanes]
    local[5].wait()

    def sweep(step):
        gr, gc = g_r[...], g_c[...]
        outer_products(a_v, gr, gc)

        def channel(ch, _):
            picks = [idx[d, ch] for d in range(4)]
            before = [prev[d, ch] for d in range(4)]
            for t in range(half // TILE):
                rows = slice(t * TILE, (t + 1) * TILE)
                below = slice(half + t * TILE, half + (t + 1) * TILE)
                re, im = residual_tile(a_v, m_v, v_v, ch, picks, rows)
                w = w_v[ch, rows, :]
                re = re.astype(BF16) * w
                im = im.astype(BF16) * w
                for d in range(4):
                    m_re = m_v[d, 0, ch, rows, :]
                    m_im = m_v[d, 1, ch, rows, :]
                    old_re = t_v[before[d], d, rows, :]
                    old_im = t_v[before[d], d, below, :]
                    t_v[ch, d, rows, :] = old_re + (re * m_re + im * m_im)
                    t_v[ch, d, below, :] = old_im + (re * m_im - im * m_re)
            return 0

        lax.fori_loop(0, chans, channel, 0)
        x_col = jnp.concatenate([gr, turned(gr)], axis=1).astype(BF16)
        x_row = gc.astype(BF16)
        at16 = rows_like((16, 2 * half))
        o_col = jnp.zeros((16, 2 * half), F32)
        o_row = jnp.zeros((16, 2 * half), F32)
        for k in range(2):
            for d in range(4):
                keep = (at16 == 8 * k + d) | (at16 == 8 * k + 4 + d)
                part = t_v[last[k, d], d]
                got = jnp.dot(x_col, part, preferred_element_type=F32)
                o_col = jnp.where(keep, got, o_col)
                got = lax.dot_general(
                    x_row, part, (((1,), (1,)), ((), ())), preferred_element_type=F32
                )
                o_row = jnp.where(keep, got, o_row)
        o_row = o_row[:, :half] - turned(o_row[:, half:])

        def squared(g):
            return jnp.concatenate(
                [g[8 * k : 8 * k + 4] ** 2 + g[8 * k + 4 : 8 * k + 8] ** 2 for k in range(2)],
                axis=0,
            )

        s_r, s_c = squared(gr), squared(gc).astype(BF16)
        at8 = rows_like(s_r.shape)
        den_c = jnp.zeros((8, 2 * half), F32)
        den_r = jnp.zeros((8, half), F32)
        for k in range(2):
            for pair in range(2):
                first = k * 4 + 2 * pair
                left = jnp.concatenate(
                    [jnp.where(at8 == first + i, s_r, 0.0) for i in range(2)], axis=1
                ).astype(BF16)
                part = d_v[k * 2 + pair]
                den_c += jnp.dot(left, part, preferred_element_type=F32)
                got = lax.dot_general(
                    s_c, part, (((1,), (1,)), ((), ())), preferred_element_type=F32
                )
                for i in range(2):
                    den_r = jnp.where(at8 == first + i, got[:, i * half : (i + 1) * half], den_r)
        colb[step, r] = jnp.concatenate([o_col, den_c], axis=0)
        rowb[step, c] = jnp.concatenate([o_row, den_r], axis=0)
        copies = []
        for k in row_list:
            copies.append(remote(
                colb.at[step, r], colb.at[step, r], col_s.at[step, k], col_r.at[step, r],
                row_peer(k),
            ))
        for k in col_list:
            copies.append(remote(
                rowb.at[step, c], rowb.at[step, c], row_s.at[step, k], row_r.at[step, c],
                col_peer(k),
            ))
        for cp in copies:
            cp.start()

        def refresh(g, total):
            den = total[16:24] + 1.0
            den = jnp.concatenate([den[0:4], den[0:4], den[4:8], den[4:8]], axis=0)
            return g + 0.5 * total[0:16] / den

        for k in row_list:
            src = lax.rem(r + k, n_row)
            remote(
                colb.at[step, src], colb.at[step, src], col_s.at[step, k], col_r.at[step, src],
                row_peer(k),
            ).wait_recv()
        total = colb[step, 0]
        for i in range(1, n_row):
            total = total + colb[step, i]
        colt[step, e] = total
        both = remote(
            colt.at[step, e], colt.at[step, e], ct_s.at[step], ct_r.at[step, e], sib
        )
        both.start()
        copies.append(both)
        for k in col_list:
            src = lax.rem(c + k, n_col)
            remote(
                rowb.at[step, src], rowb.at[step, src], row_s.at[step, k], row_r.at[step, src],
                col_peer(k),
            ).wait_recv()
        total = rowb[step, 0]
        for i in range(1, n_col):
            total = total + rowb[step, i]
        g_r[...] = refresh(gr, total)
        if step == ITERS - 1:
            g_r2[e] = g_r[...]
            rows_sib = remote(g_r2.at[e], g_r2.at[e], fin_s, fin_r.at[e], sib)
            rows_sib.start()
            copies.append(rows_sib)
        remote(
            colt.at[step, other], colt.at[step, other], ct_s.at[step], ct_r.at[step, other], sib
        ).wait_recv()
        g_c[...] = refresh(gc, colt[step, 0] + colt[step, 1])
        return copies

    copies = []
    for step in range(ITERS):
        copies += sweep(step)

    for cp in local[6:]:
        cp.wait()
    remote(
        model.at[:, :, their_ch, mine, :], mf_v.at[pl.ds(2 * other, 2)],
        mod_s.at[2], mod_r.at[2], sib,
    ).wait_recv()
    remote(g_r2.at[other], g_r2.at[other], fin_s, fin_r.at[other], sib).wait_recv()

    for cp in model_a + [model_b, gains_sib]:
        cp.wait_send()

    @pl.when(near)
    def _():
        for cp in gains_to(near_to):
            cp.wait_send()

    @pl.when(cross)
    def _():
        for cp in gains_to(cross_to):
            cp.wait_send()

    for cp in copies:
        cp.wait_send()


def finish_kernel(m_v, v_v, mf_v, vf_v, g_r2, g_c, idx, gains_out, res_out, a_v, out_v, g_v, sem, g_sem):
    e = lax.axis_index("dir")
    half = m_v.shape[3]
    fin = mf_v.shape[2]
    g = g_c[...]
    for x in range(2):
        for l in range(2):
            for k in range(2):
                at = k * 8 + x * 4 + l
                g_v[x, l, k : k + 1, :] = jnp.where(e == 0, g[at : at + 1], g[at + 2 : at + 3])
    gains_copy = pltpu.make_async_copy(g_v, gains_out, g_sem)
    gains_copy.start()
    sides = (
        (m_v, v_v, e * fin, e),
        (mf_v, vf_v, 0, 1 - e),
    )

    def moved(which, ch):
        side = sides[which][3]
        where = pl.ds(pl.multiple_of(side * half, half), half)
        return pltpu.make_async_copy(
            out_v.at[which, :, ch], res_out.at[:, ch, where, :], sem.at[which, ch]
        )

    for which, (mod, vi, base, side) in enumerate(sides):
        outer_products(a_v.at[which], g_r2[side], g)

        def channel(ch, _):
            picks = [idx[d, e * fin + ch] for d in range(4)]
            for t in range(half // TILE):
                rows = slice(t * TILE, (t + 1) * TILE)
                re, im = residual_tile(a_v.at[which], mod, vi, base + ch, picks, rows)
                out_v[which, 0, ch, rows, :] = re
                out_v[which, 1, ch, rows, :] = im
            moved(which, ch).start()
            return 0

        lax.fori_loop(0, fin, channel, 0)
    gains_copy.wait()
    for which in range(2):
        for ch in range(fin):
            moved(which, ch).wait()


def body(n_row, n_col, vis, model, gains, channel_interval_index, antenna_usable_mask):
    dirs, _, chans, rows, cols = model.shape
    half = rows // 2
    fin = chans // 2
    n_dir = 2 * dirs
    hbm = pl.BlockSpec(memory_space=pltpu.HBM)
    vmem = pl.BlockSpec(memory_space=pltpu.VMEM)
    smem = pl.BlockSpec(memory_space=pltpu.SMEM)
    dma = pltpu.SemaphoreType.DMA
    held = (
        pltpu.VMEM((n_dir, 2, chans, half, cols), BF16),
        pltpu.VMEM((2, chans, half, cols), BF16),
        pltpu.VMEM((n_dir, 2, fin, half, cols), BF16),
        pltpu.VMEM((2, fin, half, cols), BF16),
        pltpu.VMEM((2, 16, half), F32),
        pltpu.VMEM((16, cols), F32),
        pltpu.SMEM((n_dir, chans), jnp.int32),
    )
    spaces = (vmem,) * 6 + (smem,)
    args = [
        pltpu.with_memory_space_constraint(x, pltpu.HBM)
        for x in (vis, model, gains, antenna_usable_mask, channel_interval_index)
    ]
    state = pl.pallas_call(
        functools.partial(kernel, n_row, n_col),
        out_shape=held,
        in_specs=[hbm] * 5,
        out_specs=spaces,
        scratch_shapes=[
            pltpu.VMEM((chans, half, cols), BF16),
            pltpu.VMEM((4, 2 * half, cols), BF16),
            pltpu.VMEM((8, half, 2 * cols), F32),
            pltpu.VMEM((chans + 1, n_dir, 2 * half, cols), BF16),
            pltpu.VMEM((chans, half), jnp.int32),
            pltpu.VMEM((chans, cols), jnp.int32),
            pltpu.SMEM((n_dir, chans), jnp.int32),
            pltpu.SMEM((2, n_dir), jnp.int32),
            pltpu.VMEM((2,) + gains.shape, F32),
            pltpu.VMEM((2,) + gains.shape, F32),
            pltpu.VMEM((16, half), F32),
            pltpu.VMEM((ITERS, n_row, 24, cols), F32),
            pltpu.VMEM((ITERS, n_col, 24, half), F32),
            pltpu.VMEM((ITERS, 2, 24, cols), F32),
            dma((8,)),
            dma((3,)),
            dma((3,)),
            dma,
            dma,
            dma((n_col,)),
            dma((2,)),
            dma((ITERS, n_row)),
            dma((ITERS, n_row)),
            dma((ITERS, n_col)),
            dma((ITERS, n_col)),
            dma((ITERS,)),
            dma((ITERS, 2)),
            dma,
            dma((2,)),
        ],
        compiler_params=pltpu.CompilerParams(
            collective_id=0, has_side_effects=True, vmem_limit_bytes=24 * 2**20
        ),
    )(*args)
    return pl.pallas_call(
        finish_kernel,
        out_shape=(
            pltpu.HBM(gains.shape, F32),
            pltpu.HBM((2, fin, rows, cols), F32),
        ),
        in_specs=spaces,
        out_specs=(hbm, hbm),
        scratch_shapes=[
            pltpu.VMEM((2, 8, half, 2 * cols), F32),
            pltpu.VMEM((2, 2, fin, half, cols), F32),
            pltpu.VMEM(gains.shape, F32),
            dma((2, fin)),
            dma,
        ],
        compiler_params=pltpu.CompilerParams(vmem_limit_bytes=16 * 2**20),
    )(*state)


def solution(mesh):
    placed = (
        P(None, None, "row", "col"),
        P("dir", None, None, "row", "col"),
        P(None, "dir", None, "col"),
        P(),
        P(),
    )
    return jax.shard_map(
        functools.partial(body, mesh.shape["row"], mesh.shape["col"]),
        mesh=mesh,
        in_specs=placed,
        out_specs=(P(None, "dir", None, "col"), P(None, "dir", "row", "col")),
        check_vma=False,
    )
```

time: 50.7 us -> 40.2 us (0.79)
  local copies, waits for them, and re-layouts: 5.72 us -> 0 us
  Pallas kernels: 44.1 us -> 39.5 us
    unnamed x10 -> x0, local copies, waits for them, and re-layouts: 5.72 us -> none
    pallas_call x1 -> x2, Pallas kernels: 44.1 us -> 39.5 us  [the longest x1 36.1 us: body(): pl.pallas_call(functools.partial(kernel, n_row, n_col), out_shape=held, i...]
where the time goes in v2:
time: 40.2 us; the launch traced here: 40.1 us
  Pallas kernels  39.5 us (98%)
  between operations  0.64 us (2%)
    pallas_call x1, Pallas kernels, body(): pl.pallas_call(functools.partial(kernel, n_row, n_col), out_shape=held, i...  36.1 us
    pallas_call x1, Pallas kernels, body(): pl.pallas_call(finish_kernel, out_shape=(pltpu.HBM(gains.shape, F32), plt...  3.4 us

profile of v2, /device:TPU:1, one launch (start us, length us, event | category | flops | bytes accessed | tf_op | source)
XLA Modules:
  0.0 40.1 jit_solution(15115440982556764281)
XLA Ops:
  0.6 36.1 %shard_map.68 = (bf16[4,2,8,128,256]{4,3,2,1,0:T(8,128)(2,1)S(1)}, bf16[2,8,128,256]{3,2,1,0:T(8,128)(2,1)S(1)}, bf16[4,2,4,128,256]{4,3,2,1,0:T(8,128)(2,1)S(1)...) custom-call(bf16[2,8,256,256]{3,2,1,0:T(8,128)(2,1)} %vis.1, ...), custom_call_target="tpu_custom_call" | custom-call | tf_op jit(solution)/shard_map/pallas_call | solution.py:485
  36.7 3.4 %shard_map.69 = (f32[2,2,2,256]{3,2,1,0:T(2,128)}, f32[2,4,256,256]{3,2,1,0:T(8,128)}) custom-call(bf16[4,2,8,128,256]{4,3,2,1,0:T(8,128)(2,1)S(1)} %get-tuple-element.9.m_v, bf16[2,8,128,256]{3,2,1,0:T(8,128)(2,1)S(1)} %get-tuple-element.10.v_v, bf16[4,2,4,128,256]{4,3,2,1,0:T(8,128)(2,1)S(1)} %get-tuple-element.11.mf_v, ...), custom_call_target="tpu_custom_call" | custom-call | tf_op jit(solution)/shard_map/pallas_call | solution.py:525

commit v3 on v2

--- a/solution.py
+++ b/solution.py
@@ -34,17 +34,15 @@
     width = g_cols.shape[1]
     right = jnp.concatenate([g_cols, turned(g_cols)], axis=1)
     right_hi, right_lo = halves(right)
-    right_all = jnp.concatenate([right_hi, right_lo, right_hi], axis=0)
+    right_all = jnp.concatenate([right_hi, right_lo, right_hi], axis=0).astype(F32)
     left_hi, left_lo = halves(g_rows)
-    row = rows_like((48, g_rows.shape[1]))
-    left_all = jnp.concatenate([left_hi, left_hi, left_lo], axis=0).astype(F32)
+    left = jnp.concatenate([left_hi, left_hi, left_lo], axis=0).astype(F32).T.astype(BF16)
+    at = rows_like(right_all.shape) % 16
     for k in range(2):
         for d in range(4):
-            at = row % 16
             keep = (at == 8 * k + d) | (at == 8 * k + 4 + d)
-            left = jnp.where(keep, left_all, 0.0).astype(BF16)
-            a_ref[k * 4 + d] = lax.dot_general(
-                left, right_all, (((0,), (0,)), ((), ())), preferred_element_type=F32
+            a_ref[k * 4 + d] = jnp.dot(
+                left, jnp.where(keep, right_all, 0.0).astype(BF16), preferred_element_type=F32
             )
 
 
@@ -68,9 +66,9 @@
     vis, model, gains, mask, index,
     m_v, v_v, mf_v, vf_v, g_r2, g_c, idx,
     w_v, d_v, a_v, t_v, fri_v, fci_v, prev, last,
-    gin_c, gin_r, g_r, colb, rowb, colt,
+    gin_c, gin_r, g_r, coln, cold, rown, rowd, colt,
     loc_sem, mod_s, mod_r, gs_s, gs_r, gr_s, gr_r,
-    col_s, col_r, row_s, row_r, ct_s, ct_r, fin_s, fin_r,
+    cn_s, cn_r, cd_s, cd_r, rn_s, rn_r, rd_s, rd_r, ct_s, ct_r, fin_s, fin_r,
 ):
     r, c, e = lax.axis_index("row"), lax.axis_index("col"), lax.axis_index("dir")
     other = 1 - e
@@ -171,14 +169,16 @@
 
     gains_sib = remote(gin_c.at[e], gin_c.at[e], gs_s, gs_r, sib)
     gains_sib.start()
-    model_a = [
-        remote(
-            model.at[l, :, :, theirs, :], m_v.at[2 * e + l], mod_s.at[l], mod_r.at[l], sib
+
+    def chunk(ch, dirs):
+        return remote(
+            model.at[:, :, ch, theirs, :], m_v.at[dirs, :, ch], mod_s.at[ch], mod_r.at[ch], sib
         )
-        for l in range(2)
-    ]
+
+    model_a = [chunk(ch, own_dirs) for ch in range(chans)]
     model_b = remote(
-        model.at[:, :, their_ch, mine, :], mf_v.at[own_dirs], mod_s.at[2], mod_r.at[2], sib
+        model.at[:, :, their_ch, mine, :], mf_v.at[own_dirs],
+        mod_s.at[chans], mod_r.at[chans], sib,
     )
     for cp in model_a:
         cp.start()
@@ -241,12 +241,6 @@
                     at = k * 8 + x * 4 + s * 2 + l
                     g_c[at : at + 1, :] = gin_c[s, x, l, k : k + 1, :]
 
-    for l in range(2):
-        remote(
-            model.at[l, :, :, theirs, :], m_v.at[2 * other + l], mod_s.at[l], mod_r.at[l], sib
-        ).wait_recv()
-        squares(other, l)
-
     @pl.when(near)
     def _():
         gin_r[...] = gin_c[...]
@@ -267,9 +261,66 @@
 
     def sweep(step):
         gr, gc = g_r[...], g_c[...]
-        outer_products(a_v, gr, gc)
+        at16 = rows_like((16, 2 * half))
+        at8 = rows_like((8, half))
+        copies = []
+
+        def send(buf, at, sems, ks, peer):
+            for k in ks:
+                cp = remote(
+                    buf.at[step, at], buf.at[step, at], sems[0].at[step, k],
+                    sems[1].at[step, at], peer(k),
+                )
+                cp.start()
+                copies.append(cp)
+
+        def gathered(buf, sems, at, count, ks, peer):
+            for k in ks:
+                src = lax.rem(at + k, count)
+                remote(
+                    buf.at[step, src], buf.at[step, src], sems[0].at[step, k],
+                    sems[1].at[step, src], peer(k),
+                ).wait_recv()
+            total = buf[step, 0]
+            for i in range(1, count):
+                total = total + buf[step, i]
+            return total
+
+        def across(g, part):
+            return lax.dot_general(g, part, (((1,), (1,)), ((), ())), preferred_element_type=F32)
+
+        def squared(g):
+            return jnp.concatenate(
+                [g[8 * k : 8 * k + 4] ** 2 + g[8 * k + 4 : 8 * k + 8] ** 2 for k in range(2)],
+                axis=0,
+            )
+
+        def denominators():
+            s_r = squared(gr)
+            s_c = squared(gc).astype(BF16)
+            den_c = jnp.zeros((8, 2 * half), F32)
+            den_r = jnp.zeros((8, half), F32)
+            for k in range(2):
+                for pair in range(2):
+                    first = k * 4 + 2 * pair
+                    left = jnp.concatenate(
+                        [jnp.where(at8 == first + i, s_r, 0.0) for i in range(2)], axis=1
+                    ).astype(BF16)
+                    part = d_v[k * 2 + pair]
+                    den_c += jnp.dot(left, part, preferred_element_type=F32)
+                    got = across(s_c, part)
+                    for i in range(2):
+                        den_r = jnp.where(
+                            at8 == first + i, got[:, i * half : (i + 1) * half], den_r
+                        )
+            rowd[step, c] = den_r
+            send(rowd, c, (rd_s, rd_r), col_list, col_peer)
+            cold[step, r] = den_c
+            send(cold, r, (cd_s, cd_r), row_list, row_peer)
 
         def channel(ch, _):
+            if step == 0:
+                chunk(ch, pl.ds(2 * other, 2)).wait_recv()
             picks = [idx[d, ch] for d in range(4)]
             before = [prev[d, ch] for d in range(4)]
             for t in range(half // TILE):
@@ -288,93 +339,48 @@
                     t_v[ch, d, below, :] = old_im + (re * m_im - im * m_re)
             return 0
 
+        def all_parts(product):
+            out = jnp.zeros((16, 2 * half), F32)
+            for k in range(2):
+                for d in range(4):
+                    keep = (at16 == 8 * k + d) | (at16 == 8 * k + 4 + d)
+                    out = jnp.where(keep, product(t_v[last[k, d], d]), out)
+            return out
+
+        if step > 0:
+            denominators()
+        outer_products(a_v, gr, gc)
         lax.fori_loop(0, chans, channel, 0)
+        x_row = gc.astype(BF16)
         x_col = jnp.concatenate([gr, turned(gr)], axis=1).astype(BF16)
-        x_row = gc.astype(BF16)
-        at16 = rows_like((16, 2 * half))
-        o_col = jnp.zeros((16, 2 * half), F32)
-        o_row = jnp.zeros((16, 2 * half), F32)
-        for k in range(2):
-            for d in range(4):
-                keep = (at16 == 8 * k + d) | (at16 == 8 * k + 4 + d)
-                part = t_v[last[k, d], d]
-                got = jnp.dot(x_col, part, preferred_element_type=F32)
-                o_col = jnp.where(keep, got, o_col)
-                got = lax.dot_general(
-                    x_row, part, (((1,), (1,)), ((), ())), preferred_element_type=F32
-                )
-                o_row = jnp.where(keep, got, o_row)
-        o_row = o_row[:, :half] - turned(o_row[:, half:])
-
-        def squared(g):
-            return jnp.concatenate(
-                [g[8 * k : 8 * k + 4] ** 2 + g[8 * k + 4 : 8 * k + 8] ** 2 for k in range(2)],
-                axis=0,
-            )
-
-        s_r, s_c = squared(gr), squared(gc).astype(BF16)
-        at8 = rows_like(s_r.shape)
-        den_c = jnp.zeros((8, 2 * half), F32)
-        den_r = jnp.zeros((8, half), F32)
-        for k in range(2):
-            for pair in range(2):
-                first = k * 4 + 2 * pair
-                left = jnp.concatenate(
-                    [jnp.where(at8 == first + i, s_r, 0.0) for i in range(2)], axis=1
-                ).astype(BF16)
-                part = d_v[k * 2 + pair]
-                den_c += jnp.dot(left, part, preferred_element_type=F32)
-                got = lax.dot_general(
-                    s_c, part, (((1,), (1,)), ((), ())), preferred_element_type=F32
-                )
-                for i in range(2):
-                    den_r = jnp.where(at8 == first + i, got[:, i * half : (i + 1) * half], den_r)
-        colb[step, r] = jnp.concatenate([o_col, den_c], axis=0)
-        rowb[step, c] = jnp.concatenate([o_row, den_r], axis=0)
-        copies = []
-        for k in row_list:
-            copies.append(remote(
-                colb.at[step, r], colb.at[step, r], col_s.at[step, k], col_r.at[step, r],
-                row_peer(k),
-            ))
-        for k in col_list:
-            copies.append(remote(
-                rowb.at[step, c], rowb.at[step, c], row_s.at[step, k], row_r.at[step, c],
-                col_peer(k),
-            ))
-        for cp in copies:
-            cp.start()
-
-        def refresh(g, total):
-            den = total[16:24] + 1.0
+        o_row = all_parts(lambda part: across(x_row, part))
+        rown[step, c] = o_row[:, :half] - turned(o_row[:, half:])
+        send(rown, c, (rn_s, rn_r), col_list, col_peer)
+        coln[step, r] = all_parts(
+            lambda part: jnp.dot(x_col, part, preferred_element_type=F32)
+        )
+        send(coln, r, (cn_s, cn_r), row_list, row_peer)
+        if step == 0:
+            for l in range(2):
+                squares(other, l)
+            denominators()
+
+        def refresh(g, total, den):
+            den = den + 1.0
             den = jnp.concatenate([den[0:4], den[0:4], den[4:8], den[4:8]], axis=0)
-            return g + 0.5 * total[0:16] / den
-
-        for k in row_list:
-            src = lax.rem(r + k, n_row)
-            remote(
-                colb.at[step, src], colb.at[step, src], col_s.at[step, k], col_r.at[step, src],
-                row_peer(k),
-            ).wait_recv()
-        total = colb[step, 0]
-        for i in range(1, n_row):
-            total = total + colb[step, i]
-        colt[step, e] = total
+            return g + 0.5 * total / den
+
+        total = gathered(coln, (cn_s, cn_r), r, n_row, row_list, row_peer)
+        total_den = gathered(cold, (cd_s, cd_r), r, n_row, row_list, row_peer)
+        colt[step, e] = jnp.concatenate([total, total_den], axis=0)
         both = remote(
             colt.at[step, e], colt.at[step, e], ct_s.at[step], ct_r.at[step, e], sib
         )
         both.start()
         copies.append(both)
-        for k in col_list:
-            src = lax.rem(c + k, n_col)
-            remote(
-                rowb.at[step, src], rowb.at[step, src], row_s.at[step, k], row_r.at[step, src],
-                col_peer(k),
-            ).wait_recv()
-        total = rowb[step, 0]
-        for i in range(1, n_col):
-            total = total + rowb[step, i]
-        g_r[...] = refresh(gr, total)
+        total = gathered(rown, (rn_s, rn_r), c, n_col, col_list, col_peer)
+        total_den = gathered(rowd, (rd_s, rd_r), c, n_col, col_list, col_peer)
+        g_r[...] = refresh(gr, total, total_den)
         if step == ITERS - 1:
             g_r2[e] = g_r[...]
             rows_sib = remote(g_r2.at[e], g_r2.at[e], fin_s, fin_r.at[e], sib)
@@ -383,7 +389,8 @@
         remote(
             colt.at[step, other], colt.at[step, other], ct_s.at[step], ct_r.at[step, other], sib
         ).wait_recv()
-        g_c[...] = refresh(gc, colt[step, 0] + colt[step, 1])
+        total = colt[step, 0] + colt[step, 1]
+        g_c[...] = refresh(gc, total[0:16], total[16:24])
         return copies
 
     copies = []
@@ -394,7 +401,7 @@
         cp.wait()
     remote(
         model.at[:, :, their_ch, mine, :], mf_v.at[pl.ds(2 * other, 2)],
-        mod_s.at[2], mod_r.at[2], sib,
+        mod_s.at[chans], mod_r.at[chans], sib,
     ).wait_recv()
     remote(g_r2.at[other], g_r2.at[other], fin_s, fin_r.at[other], sib).wait_recv()
 
@@ -499,18 +506,24 @@
             pltpu.VMEM((2,) + gains.shape, F32),
             pltpu.VMEM((2,) + gains.shape, F32),
             pltpu.VMEM((16, half), F32),
-            pltpu.VMEM((ITERS, n_row, 24, cols), F32),
-            pltpu.VMEM((ITERS, n_col, 24, half), F32),
+            pltpu.VMEM((ITERS, n_row, 16, cols), F32),
+            pltpu.VMEM((ITERS, n_row, 8, cols), F32),
+            pltpu.VMEM((ITERS, n_col, 16, half), F32),
+            pltpu.VMEM((ITERS, n_col, 8, half), F32),
             pltpu.VMEM((ITERS, 2, 24, cols), F32),
             dma((8,)),
-            dma((3,)),
-            dma((3,)),
+            dma((chans + 1,)),
+            dma((chans + 1,)),
             dma,
             dma,
             dma((n_col,)),
             dma((2,)),
             dma((ITERS, n_row)),
             dma((ITERS, n_row)),
+            dma((ITERS, n_row)),
+            dma((ITERS, n_row)),
+            dma((ITERS, n_col)),
+            dma((ITERS, n_col)),
             dma((ITERS, n_col)),
             dma((ITERS, n_col)),
             dma((ITERS,)),

time: 40.2 us -> 37.6 us (0.935)
  Pallas kernels: 39.5 us -> 36.9 us
    pallas_call x1, Pallas kernels: 36.1 us -> 33.4 us  [body(): pl.pallas_call(functools.partial(kernel, n_row, n_col), out_shape=held, i...]
where the time goes in v3:
time: 37.6 us; the launch traced here: 37.5 us
  Pallas kernels  36.9 us (98%)
  between operations  0.64 us (2%)
    pallas_call x1, Pallas kernels, body(): pl.pallas_call(functools.partial(kernel, n_row, n_col), out_shape=held, i...  33.4 us
    pallas_call x1, Pallas kernels, body(): pl.pallas_call(finish_kernel, out_shape=(pltpu.HBM(gains.shape, F32), plt...  3.44 us

profile of v3, /device:TPU:1, one launch (start us, length us, event | category | flops | bytes accessed | tf_op | source)
XLA Modules:
  0.0 37.5 jit_solution(17796994809596422151)
XLA Ops:
  0.6 33.4 %shard_map.68 = (bf16[4,2,8,128,256]{4,3,2,1,0:T(8,128)(2,1)S(1)}, bf16[2,8,128,256]{3,2,1,0:T(8,128)(2,1)S(1)}, bf16[4,2,4,128,256]{4,3,2,1,0:T(8,128)(2,1)S(1)...) custom-call(bf16[2,8,256,256]{3,2,1,0:T(8,128)(2,1)} %vis.1, ...), custom_call_target="tpu_custom_call" | custom-call | tf_op jit(solution)/shard_map/pallas_call | solution.py:492
  34.1 3.4 %shard_map.69 = (f32[2,2,2,256]{3,2,1,0:T(2,128)}, f32[2,4,256,256]{3,2,1,0:T(8,128)}) custom-call(bf16[4,2,8,128,256]{4,3,2,1,0:T(8,128)(2,1)S(1)} %get-tuple-element.9.m_v, bf16[2,8,128,256]{3,2,1,0:T(8,128)(2,1)S(1)} %get-tuple-element.10.v_v, bf16[4,2,4,128,256]{4,3,2,1,0:T(8,128)(2,1)S(1)} %get-tuple-element.11.mf_v, ...), custom_call_target="tpu_custom_call" | custom-call | tf_op jit(solution)/shard_map/pallas_call | solution.py:538

commit v4 on v3

--- a/solution.py
+++ b/solution.py
@@ -66,8 +66,8 @@
     vis, model, gains, mask, index,
     m_v, v_v, mf_v, vf_v, g_r2, g_c, idx,
     w_v, d_v, a_v, t_v, fri_v, fci_v, prev, last,
-    gin_c, gin_r, g_r, coln, cold, rown, rowd, colt,
-    loc_sem, mod_s, mod_r, gs_s, gs_r, gr_s, gr_r,
+    gin_c, gin_r, g_r, coln, cold, rown, rowd, colns, colds, rowns, colt,
+    late, loc_sem, mod_s, mod_r, gs_s, gs_r, gr_s, gr_r,
     cn_s, cn_r, cd_s, cd_r, rn_s, rn_r, rd_s, rd_r, ct_s, ct_r, fin_s, fin_r,
 ):
     r, c, e = lax.axis_index("row"), lax.axis_index("col"), lax.axis_index("dir")
@@ -110,10 +110,20 @@
                 barrier, inc=1, device_id=(source_row, r, x), device_id_type=MESH
             )
 
+    holder = near | cross
+    partners = []
     for k in col_list:
-        pl.semaphore_signal(barrier, inc=1, device_id=col_peer(k), device_id_type=MESH)
+        to = col_peer(k)
+        partners.append((to, (to[1] == r) | (to[1] == flip_r)))
     for k in row_list:
-        pl.semaphore_signal(barrier, inc=1, device_id=row_peer(k), device_id_type=MESH)
+        to = row_peer(k)
+        partners.append((to, (to[0] == c) | (to[0] == flip_c)))
+    for to, holds in partners:
+
+        @pl.when(holder | jnp.logical_not(holds))
+        def _(to=to):
+            pl.semaphore_signal(barrier, inc=1, device_id=to, device_id_type=MESH)
+
     pl.semaphore_signal(barrier, inc=1, device_id=sib, device_id_type=MESH)
 
     mine = pl.ds(pl.multiple_of(e * half, half), half)
@@ -147,7 +157,7 @@
     n_near, n_cross = len(near_to), len(cross_to)
     pl.semaphore_wait(
         barrier,
-        len(col_list) + len(row_list) + 1
+        jnp.where(holder, 2, len(partners)) + 1
         + jnp.where(near, n_near, 0) + jnp.where(cross, n_cross, 0),
     )
 
@@ -183,6 +193,12 @@
     for cp in model_a:
         cp.start()
     model_b.start()
+
+    for to, holds in partners:
+
+        @pl.when(jnp.logical_not(holder) & holds)
+        def _(to=to):
+            pl.semaphore_signal(late, inc=1, device_id=to, device_id_type=MESH)
 
     for cp in local[1:4]:
         cp.wait()
@@ -259,8 +275,9 @@
                     g_r[at : at + 1, :] = gin_r[s, x, l, k : k + 1, lanes]
     local[5].wait()
 
-    def sweep(step):
+    def sweep(step, error):
         gr, gc = g_r[...], g_c[...]
+        short = step == 0
         at16 = rows_like((16, 2 * half))
         at8 = rows_like((8, half))
         copies = []
@@ -281,9 +298,9 @@
                     buf.at[step, src], buf.at[step, src], sems[0].at[step, k],
                     sems[1].at[step, src], peer(k),
                 ).wait_recv()
-            total = buf[step, 0]
+            total = buf[step, 0].astype(F32)
             for i in range(1, count):
-                total = total + buf[step, i]
+                total = total + buf[step, i].astype(F32)
             return total
 
         def across(g, part):
@@ -315,8 +332,14 @@
                         )
             rowd[step, c] = den_r
             send(rowd, c, (rd_s, rd_r), col_list, col_peer)
+            if short:
+                den_16 = den_c.astype(BF16)
+                colds[step, r] = jnp.concatenate([den_16[:, :half], den_16[:, half:]], axis=0)
+                send(colds, r, (cd_s, cd_r), row_list, row_peer)
+                return den_c - den_16.astype(F32)
             cold[step, r] = den_c
             send(cold, r, (cd_s, cd_r), row_list, row_peer)
+            return None
 
         def channel(ch, _):
             if step == 0:
@@ -351,36 +374,52 @@
             denominators()
         outer_products(a_v, gr, gc)
         lax.fori_loop(0, chans, channel, 0)
+        if step == 0:
+
+            @pl.when(holder)
+            def _():
+                pl.semaphore_wait(late, len(partners) - 2)
+
         x_row = gc.astype(BF16)
         x_col = jnp.concatenate([gr, turned(gr)], axis=1).astype(BF16)
         o_row = all_parts(lambda part: across(x_row, part))
-        rown[step, c] = o_row[:, :half] - turned(o_row[:, half:])
-        send(rown, c, (rn_s, rn_r), col_list, col_peer)
-        coln[step, r] = all_parts(
-            lambda part: jnp.dot(x_col, part, preferred_element_type=F32)
-        )
-        send(coln, r, (cn_s, cn_r), row_list, row_peer)
-        if step == 0:
+        o_row = o_row[:, :half] - turned(o_row[:, half:])
+        if short:
+            rowns[step, c] = o_row.astype(BF16)
+            send(rowns, c, (rn_s, rn_r), col_list, col_peer)
+        else:
+            rown[step, c] = o_row + error[0]
+            send(rown, c, (rn_s, rn_r), col_list, col_peer)
+        o_col = all_parts(lambda part: jnp.dot(x_col, part, preferred_element_type=F32))
+        if short:
+            colns[step, r] = o_col.astype(BF16)
+            send(colns, r, (cn_s, cn_r), row_list, row_peer)
             for l in range(2):
                 squares(other, l)
-            denominators()
-
-        def refresh(g, total, den):
+            lost_den = denominators()
+        else:
+            coln[step, r] = o_col + error[1]
+            send(coln, r, (cn_s, cn_r), row_list, row_peer)
+
+        def refresh(total, den):
             den = den + 1.0
             den = jnp.concatenate([den[0:4], den[0:4], den[4:8], den[4:8]], axis=0)
-            return g + 0.5 * total / den
-
-        total = gathered(coln, (cn_s, cn_r), r, n_row, row_list, row_peer)
-        total_den = gathered(cold, (cd_s, cd_r), r, n_row, row_list, row_peer)
+            return 0.5 * total / den
+
+        total = gathered(colns if short else coln, (cn_s, cn_r), r, n_row, row_list, row_peer)
+        total_den = gathered(colds if short else cold, (cd_s, cd_r), r, n_row, row_list, row_peer)
+        if short:
+            total_den = jnp.concatenate([total_den[0:8], total_den[8:16]], axis=1)
         colt[step, e] = jnp.concatenate([total, total_den], axis=0)
         both = remote(
             colt.at[step, e], colt.at[step, e], ct_s.at[step], ct_r.at[step, e], sib
         )
         both.start()
         copies.append(both)
-        total = gathered(rown, (rn_s, rn_r), c, n_col, col_list, col_peer)
+        total = gathered(rowns if short else rown, (rn_s, rn_r), c, n_col, col_list, col_peer)
         total_den = gathered(rowd, (rd_s, rd_r), c, n_col, col_list, col_peer)
-        g_r[...] = refresh(gr, total, total_den)
+        change_r = refresh(total, total_den)
+        g_r[...] = gr + change_r
         if step == ITERS - 1:
             g_r2[e] = g_r[...]
             rows_sib = remote(g_r2.at[e], g_r2.at[e], fin_s, fin_r.at[e], sib)
@@ -390,12 +429,21 @@
             colt.at[step, other], colt.at[step, other], ct_s.at[step], ct_r.at[step, other], sib
         ).wait_recv()
         total = colt[step, 0] + colt[step, 1]
-        g_c[...] = refresh(gc, total[0:16], total[16:24])
-        return copies
-
-    copies = []
+        change_c = refresh(total[0:16], total[16:24])
+        g_c[...] = gc + change_c
+        if short:
+            lost_r = o_row - rowns[step, c].astype(F32)
+            lost_c = o_col - colns[step, r].astype(F32)
+            lost_den = jnp.concatenate(
+                [lost_den[0:4], lost_den[0:4], lost_den[4:8], lost_den[4:8]], axis=0
+            )
+            error = (0.5 * lost_r, 0.5 * lost_c - change_c * lost_den)
+        return copies, error
+
+    copies, error = [], None
     for step in range(ITERS):
-        copies += sweep(step)
+        started, error = sweep(step, error)
+        copies += started
 
     for cp in local[6:]:
         cp.wait()
@@ -449,7 +497,7 @@
     for which, (mod, vi, base, side) in enumerate(sides):
         outer_products(a_v.at[which], g_r2[side], g)
 
-        def channel(ch, _):
+        for ch in range(fin):
             picks = [idx[d, e * fin + ch] for d in range(4)]
             for t in range(half // TILE):
                 rows = slice(t * TILE, (t + 1) * TILE)
@@ -457,9 +505,6 @@
                 out_v[which, 0, ch, rows, :] = re
                 out_v[which, 1, ch, rows, :] = im
             moved(which, ch).start()
-            return 0
-
-        lax.fori_loop(0, fin, channel, 0)
     gains_copy.wait()
     for which in range(2):
         for ch in range(fin):
@@ -510,7 +555,11 @@
             pltpu.VMEM((ITERS, n_row, 8, cols), F32),
             pltpu.VMEM((ITERS, n_col, 16, half), F32),
             pltpu.VMEM((ITERS, n_col, 8, half), F32),
+            pltpu.VMEM((1, n_row, 16, cols), BF16),
+            pltpu.VMEM((1, n_row, 16, half), BF16),
+            pltpu.VMEM((1, n_col, 16, half), BF16),
             pltpu.VMEM((ITERS, 2, 24, cols), F32),
+            pltpu.SemaphoreType.REGULAR,
             dma((8,)),
             dma((chans + 1,)),
             dma((chans + 1,)),

time: 37.6 us -> 35.8 us (0.952)
  Pallas kernels: 36.9 us -> 35.1 us
    pallas_call x1, Pallas kernels: 33.4 us -> 32.1 us  [body(): pl.pallas_call(functools.partial(kernel, n_row, n_col), out_shape=held, i...]
    pallas_call x1, Pallas kernels: 3.44 us -> 2.91 us  [body(): pl.pallas_call(finish_kernel, out_shape=(pltpu.HBM(gains.shape, F32), plt...]
where the time goes in v4:
time: 35.8 us; the launch traced here: 35.7 us
  Pallas kernels  35.1 us (98%)
  between operations  0.64 us (2%)
    pallas_call x1, Pallas kernels, body(): pl.pallas_call(functools.partial(kernel, n_row, n_col), out_shape=held, i...  32.1 us
    pallas_call x1, Pallas kernels, body(): pl.pallas_call(finish_kernel, out_shape=(pltpu.HBM(gains.shape, F32), plt...  2.91 us

profile of v4, /device:TPU:1, one launch (start us, length us, event | category | flops | bytes accessed | tf_op | source)
XLA Modules:
  0.0 35.7 jit_solution(14492696924644422402)
XLA Ops:
  0.6 32.1 %shard_map.68 = (bf16[4,2,8,128,256]{4,3,2,1,0:T(8,128)(2,1)S(1)}, bf16[2,8,128,256]{3,2,1,0:T(8,128)(2,1)S(1)}, bf16[4,2,4,128,256]{4,3,2,1,0:T(8,128)(2,1)S(1)...) custom-call(bf16[2,8,256,256]{3,2,1,0:T(8,128)(2,1)} %vis.1, ...), custom_call_target="tpu_custom_call" | custom-call | tf_op jit(solution)/shard_map/pallas_call | solution.py:537
  32.8 2.9 %shard_map.69 = (f32[2,2,2,256]{3,2,1,0:T(2,128)}, f32[2,4,256,256]{3,2,1,0:T(8,128)}) custom-call(bf16[4,2,8,128,256]{4,3,2,1,0:T(8,128)(2,1)S(1)} %get-tuple-element.9.m_v, bf16[2,8,128,256]{3,2,1,0:T(8,128)(2,1)S(1)} %get-tuple-element.10.v_v, bf16[4,2,4,128,256]{4,3,2,1,0:T(8,128)(2,1)S(1)} %get-tuple-element.11.mf_v, ...), custom_call_target="tpu_custom_call" | custom-call | tf_op jit(solution)/shard_map/pallas_call | solution.py:587

commit v5 on v4

--- a/solution.py
+++ b/solution.py
@@ -31,24 +31,30 @@
 
 
 def outer_products(a_ref, g_rows, g_cols):
-    width = g_cols.shape[1]
-    right = jnp.concatenate([g_cols, turned(g_cols)], axis=1)
-    right_hi, right_lo = halves(right)
-    right_all = jnp.concatenate([right_hi, right_lo, right_hi], axis=0).astype(F32)
+    count, width = g_rows.shape[1], g_cols.shape[1]
+    right_hi, right_lo = halves(jnp.concatenate([g_cols, turned(g_cols)], axis=1))
+    right = jnp.concatenate([right_hi, right_lo, right_hi], axis=0)
     left_hi, left_lo = halves(g_rows)
-    left = jnp.concatenate([left_hi, left_hi, left_lo], axis=0).astype(F32).T.astype(BF16)
-    at = rows_like(right_all.shape) % 16
-    for k in range(2):
-        for d in range(4):
-            keep = (at == 8 * k + d) | (at == 8 * k + 4 + d)
-            a_ref[k * 4 + d] = jnp.dot(
-                left, jnp.where(keep, right_all, 0.0).astype(BF16), preferred_element_type=F32
-            )
-
-
-def residual_tile(a, mod, vi, ch, picks, rows):
-    re = vi[0, ch, rows, :].astype(F32)
-    im = vi[1, ch, rows, :].astype(F32)
+    left = jnp.concatenate([left_hi, left_hi, left_lo], axis=0).astype(F32).T
+    lane = lax.broadcasted_iota(jnp.int32, left.shape, 1) % 16
+    across = g_rows.T
+    for d in range(4):
+        keep = (lane == d) | (lane == 4 + d)
+        a_ref[d] = jnp.dot(
+            jnp.where(keep, left, 0.0).astype(BF16), right, preferred_element_type=F32
+        )
+        q_re, q_im = g_cols[8 + d : 9 + d, :], g_cols[12 + d : 13 + d, :]
+        for t in range(count // 8):
+            rows = slice(t * 8, (t + 1) * 8)
+            p_re, p_im = across[rows, 8 + d : 9 + d], across[rows, 12 + d : 13 + d]
+            a_ref[4 + d, rows, 0:width] = p_re * q_re + p_im * q_im
+            a_ref[4 + d, rows, width : 2 * width] = p_im * q_re - p_re * q_im
+
+
+def residual_tile(a, mod, vi, ch, picks, rows, vi_ch=None):
+    vi_ch = ch if vi_ch is None else vi_ch
+    re = vi[0, vi_ch, rows, :].astype(F32)
+    im = vi[1, vi_ch, rows, :].astype(F32)
     width = re.shape[1]
     for d in range(4):
         at = picks[d] * 4 + d
@@ -64,8 +70,8 @@
 def kernel(
     n_row, n_col,
     vis, model, gains, mask, index,
-    m_v, v_v, mf_v, vf_v, g_r2, g_c, idx,
-    w_v, d_v, a_v, t_v, fri_v, fci_v, prev, last,
+    m_w, mf_w, v_w, g_r2, g_c, idx,
+    m_v, v_v, mf_v, vf_v, w_v, d_v, a_v, t_v, fri_v, fci_v, prev, last,
     gin_c, gin_r, g_r, coln, cold, rown, rowd, colns, colds, rowns, colt,
     late, loc_sem, mod_s, mod_r, gs_s, gs_r, gr_s, gr_r,
     cn_s, cn_r, cd_s, cd_r, rn_s, rn_r, rd_s, rd_r, ct_s, ct_r, fin_s, fin_r,
@@ -274,6 +280,22 @@
                     at = k * 8 + x * 4 + s * 2 + l
                     g_r[at : at + 1, :] = gin_r[s, x, l, k : k + 1, lanes]
     local[5].wait()
+
+    def widen(pairs):
+        for dst, src in pairs:
+            for t in range(half // (2 * TILE)):
+                rows = slice(t * 2 * TILE, (t + 1) * 2 * TILE)
+                dst[rows, :] = src[rows, :].astype(F32)
+
+    def widen_model(ch, _):
+        widen([(m_w.at[d, x, ch], m_v.at[d, x, ch]) for d in range(4) for x in range(2)])
+        return 0
+
+    def widen_rest(ch, _):
+        widen([(mf_w.at[d, x, ch], mf_v.at[d, x, ch]) for d in range(4) for x in range(2)])
+        widen([(v_w.at[0, x, ch], v_v.at[x, e * fin + ch]) for x in range(2)])
+        widen([(v_w.at[1, x, ch], vf_v.at[x, ch]) for x in range(2)])
+        return 0
 
     def sweep(step, error):
         gr, gc = g_r[...], g_c[...]
@@ -349,7 +371,7 @@
             for t in range(half // TILE):
                 rows = slice(t * TILE, (t + 1) * TILE)
                 below = slice(half + t * TILE, half + (t + 1) * TILE)
-                re, im = residual_tile(a_v, m_v, v_v, ch, picks, rows)
+                re, im = residual_tile(a_v, m_v if short else m_w, v_v, ch, picks, rows)
                 w = w_v[ch, rows, :]
                 re = re.astype(BF16) * w
                 im = im.astype(BF16) * w
@@ -397,9 +419,17 @@
             for l in range(2):
                 squares(other, l)
             lost_den = denominators()
+            lax.fori_loop(0, chans, widen_model, 0)
         else:
             coln[step, r] = o_col + error[1]
             send(coln, r, (cn_s, cn_r), row_list, row_peer)
+            for cp in local[6:]:
+                cp.wait()
+            remote(
+                model.at[:, :, their_ch, mine, :], mf_v.at[pl.ds(2 * other, 2)],
+                mod_s.at[chans], mod_r.at[chans], sib,
+            ).wait_recv()
+            lax.fori_loop(0, fin, widen_rest, 0)
 
         def refresh(total, den):
             den = den + 1.0
@@ -445,12 +475,6 @@
         started, error = sweep(step, error)
         copies += started
 
-    for cp in local[6:]:
-        cp.wait()
-    remote(
-        model.at[:, :, their_ch, mine, :], mf_v.at[pl.ds(2 * other, 2)],
-        mod_s.at[chans], mod_r.at[chans], sib,
-    ).wait_recv()
     remote(g_r2.at[other], g_r2.at[other], fin_s, fin_r.at[other], sib).wait_recv()
 
     for cp in model_a + [model_b, gains_sib]:
@@ -470,10 +494,10 @@
         cp.wait_send()
 
 
-def finish_kernel(m_v, v_v, mf_v, vf_v, g_r2, g_c, idx, gains_out, res_out, a_v, out_v, g_v, sem, g_sem):
+def finish_kernel(m_w, mf_w, v_w, g_r2, g_c, idx, gains_out, res_out, a_v, out_v, g_v, sem, g_sem):
     e = lax.axis_index("dir")
-    half = m_v.shape[3]
-    fin = mf_v.shape[2]
+    half = m_w.shape[3]
+    fin = mf_w.shape[2]
     g = g_c[...]
     for x in range(2):
         for l in range(2):
@@ -483,8 +507,8 @@
     gains_copy = pltpu.make_async_copy(g_v, gains_out, g_sem)
     gains_copy.start()
     sides = (
-        (m_v, v_v, e * fin, e),
-        (mf_v, vf_v, 0, 1 - e),
+        (m_w, v_w.at[0], e * fin, e),
+        (mf_w, v_w.at[1], 0, 1 - e),
     )
 
     def moved(which, ch):
@@ -501,7 +525,7 @@
             picks = [idx[d, e * fin + ch] for d in range(4)]
             for t in range(half // TILE):
                 rows = slice(t * TILE, (t + 1) * TILE)
-                re, im = residual_tile(a_v.at[which], mod, vi, base + ch, picks, rows)
+                re, im = residual_tile(a_v.at[which], mod, vi, base + ch, picks, rows, ch)
                 out_v[which, 0, ch, rows, :] = re
                 out_v[which, 1, ch, rows, :] = im
             moved(which, ch).start()
@@ -521,15 +545,14 @@
     smem = pl.BlockSpec(memory_space=pltpu.SMEM)
     dma = pltpu.SemaphoreType.DMA
     held = (
-        pltpu.VMEM((n_dir, 2, chans, half, cols), BF16),
-        pltpu.VMEM((2, chans, half, cols), BF16),
-        pltpu.VMEM((n_dir, 2, fin, half, cols), BF16),
-        pltpu.VMEM((2, fin, half, cols), BF16),
+        pltpu.VMEM((n_dir, 2, chans, half, cols), F32),
+        pltpu.VMEM((n_dir, 2, fin, half, cols), F32),
+        pltpu.VMEM((2, 2, fin, half, cols), F32),
         pltpu.VMEM((2, 16, half), F32),
         pltpu.VMEM((16, cols), F32),
         pltpu.SMEM((n_dir, chans), jnp.int32),
     )
-    spaces = (vmem,) * 6 + (smem,)
+    spaces = (vmem,) * 5 + (smem,)
     args = [
         pltpu.with_memory_space_constraint(x, pltpu.HBM)
         for x in (vis, model, gains, antenna_usable_mask, channel_interval_index)
@@ -540,6 +563,10 @@
         in_specs=[hbm] * 5,
         out_specs=spaces,
         scratch_shapes=[
+            pltpu.VMEM((n_dir, 2, chans, half, cols), BF16),
+            pltpu.VMEM((2, chans, half, cols), BF16),
+            pltpu.VMEM((n_dir, 2, fin, half, cols), BF16),
+            pltpu.VMEM((2, fin, half, cols), BF16),
             pltpu.VMEM((chans, half, cols), BF16),
             pltpu.VMEM((4, 2 * half, cols), BF16),
             pltpu.VMEM((8, half, 2 * cols), F32),
@@ -581,7 +608,7 @@
             dma((2,)),
         ],
         compiler_params=pltpu.CompilerParams(
-            collective_id=0, has_side_effects=True, vmem_limit_bytes=24 * 2**20
+            collective_id=0, has_side_effects=True, vmem_limit_bytes=28 * 2**20
         ),
     )(*args)
     return pl.pallas_call(

time: 35.8 us -> 35 us (0.978)
  Pallas kernels: 35.1 us -> 34.3 us
    pallas_call x1, Pallas kernels: 32.1 us -> 31.7 us  [body(): pl.pallas_call(functools.partial(kernel, n_row, n_col), out_shape=held, i...]
where the time goes in v5:
time: 35 us; the launch traced here: 34.9 us
  Pallas kernels  34.3 us (98%)
  between operations  0.64 us (2%)
    pallas_call x1, Pallas kernels, body(): pl.pallas_call(functools.partial(kernel, n_row, n_col), out_shape=held, i...  31.7 us
    pallas_call x1, Pallas kernels, body(): pl.pallas_call(finish_kernel, out_shape=(pltpu.HBM(gains.shape, F32), plt...  2.62 us

profile of v5, /device:TPU:1, one launch (start us, length us, event | category | flops | bytes accessed | tf_op | source)
XLA Modules:
  0.0 34.9 jit_solution(7237012927791819616)
XLA Ops:
  0.6 31.7 %shard_map.68 = (f32[4,2,8,128,256]{4,3,2,1,0:T(8,128)S(1)}, f32[4,2,4,128,256]{4,3,2,1,0:T(8,128)S(1)}, f32[2,2,4,128,256]{4,3,2,1,0:T(8,128)S(1)}, f32[2,16,12...) custom-call(bf16[2,8,256,256]{3,2,1,0:T(8,128)(2,1)} %vis.1, bf16[2,2,8,256,256]{4,3,2,1,0:T(8,128)(2,1)} %model.1, ...), custom_call_target="tpu_custom_call" | custom-call | tf_op jit(solution)/shard_map/pallas_call | solution.py:560
  32.3 2.6 %shard_map.69 = (f32[2,2,2,256]{3,2,1,0:T(2,128)}, f32[2,4,256,256]{3,2,1,0:T(8,128)}) custom-call(f32[4,2,8,128,256]{4,3,2,1,0:T(8,128)S(1)} %get-tuple-element.8.m_w, f32[4,2,4,128,256]{4,3,2,1,0:T(8,128)S(1)} %get-tuple-element.9.mf_w, f32[2,2,4,128,256]{4,3,2,1,0:T(8,128)S(1)} %get-tuple-element.10.v_w, f32[2,16,128]{2,1,0:T(8,128)S(1)} %get-tuple-element.11.g_r2, ...), custom_call_target="tpu_custom_call" | custom-call | tf_op jit(solution)/shard_map/pallas_call | solution.py:614

commit v6 on v5

--- a/solution.py
+++ b/solution.py
@@ -71,10 +71,10 @@
     n_row, n_col,
     vis, model, gains, mask, index,
     m_w, mf_w, v_w, g_r2, g_c, idx,
-    m_v, v_v, mf_v, vf_v, w_v, d_v, a_v, t_v, fri_v, fci_v, prev, last,
-    gin_c, gin_r, g_r, coln, cold, rown, rowd, colns, colds, rowns, colt,
+    m_v, v_v, mf_v, vf_v, mo_v, w_v, wo_v, d_v, d0_v, a_v, t_v, fri_v, fro_v, fci_v, prev, last,
+    gin_c, gin_r, g_r, coln, cold, rown, rowd, colns, colds, rowns, rowds, dens, g_f, colt,
     late, loc_sem, mod_s, mod_r, gs_s, gs_r, gr_s, gr_r,
-    cn_s, cn_r, cd_s, cd_r, rn_s, rn_r, rd_s, rd_r, ct_s, ct_r, fin_s, fin_r,
+    cn_s, cn_r, cd_s, cd_r, rn_s, rn_r, rd_s, rd_r, ct_s, ct_r, ds_s, ds_r, fin_s, fin_r,
 ):
     r, c, e = lax.axis_index("row"), lax.axis_index("col"), lax.axis_index("dir")
     other = 1 - e
@@ -137,6 +137,7 @@
     my_ch = pl.ds(e * fin, fin)
     their_ch = pl.ds(other * fin, fin)
     block_r = pl.ds(pl.multiple_of(r * 2 * half + e * half, half), half)
+    block_o = pl.ds(pl.multiple_of(r * 2 * half + other * half, half), half)
     block_c = pl.ds(pl.multiple_of(c * 2 * half, 2 * half), 2 * half)
     own_dirs = pl.ds(2 * e, 2)
     local = [
@@ -148,6 +149,8 @@
         (vis.at[:, :, mine, :], v_v),
         (vis.at[:, my_ch, theirs, :], vf_v),
         (model.at[:, :, my_ch, theirs, :], mf_v.at[own_dirs]),
+        (mask.at[:, block_o], fro_v),
+        (model.at[:, :, :, theirs, :], mo_v),
     ]
     local = [pltpu.make_async_copy(s, d, loc_sem.at[i]) for i, (s, d) in enumerate(local)]
     for cp in local:
@@ -217,43 +220,61 @@
         for k in range(2):
             last[k, d] = ends[k]
     t_v[chans] = jnp.zeros(t_v.shape[1:], BF16)
+    local[8].wait()
     shape = (half, 2 * half)
-    p_at = r * 2 * half + e * half + rows_like(shape)
     q_at = c * 2 * half + lax.broadcasted_iota(jnp.int32, shape, 1)
-    apart = p_at != q_at
-    f_r = fri_v[...].astype(F32)
     f_c = fci_v[...].astype(F32).astype(BF16)
-    for ch in range(chans):
-        one = jnp.where(rows_like(f_r.shape) == ch, f_r, 0.0).astype(BF16)
-        both = lax.dot_general(
-            one, f_c, (((0,), (0,)), ((), ())), preferred_element_type=F32
-        )
-        w_v[ch] = jnp.where(apart, both, 0.0).astype(BF16)
-
-    def squares(core, l):
-        d = 2 * core + l
-
+    for side, flags, out in ((e, fri_v, w_v), (other, fro_v, wo_v)):
+        apart = r * 2 * half + side * half + rows_like(shape) != q_at
+        f_r = flags[...].astype(F32)
+        for ch in range(chans):
+            one = jnp.where(rows_like(f_r.shape) == ch, f_r, 0.0).astype(BF16)
+            both = lax.dot_general(
+                one, f_c, (((0,), (0,)), ((), ())), preferred_element_type=F32
+            )
+            out[ch] = jnp.where(apart, both, 0.0).astype(BF16)
+
+    def square_sums(mod, d, l, weights, store):
         def tile(t, _):
             at = pl.multiple_of(t * TILE, TILE)
             rows = pl.ds(at, TILE)
             total = [jnp.zeros((TILE, 2 * half), F32)] * 2
             for ch in range(chans):
-                re = m_v[d, 0, ch, rows, :].astype(F32)
-                im = m_v[d, 1, ch, rows, :].astype(F32)
-                sq = (re * re + im * im) * w_v[ch, rows, :].astype(F32)
-                second = idx[d, ch].astype(F32)
-                part = sq * second
+                re = mod[l, 0, ch, rows, :].astype(F32)
+                im = mod[l, 1, ch, rows, :].astype(F32)
+                sq = (re * re + im * im) * weights[ch, rows, :].astype(F32)
+                part = sq * idx[d, ch].astype(F32)
                 total = [total[0] + sq, total[1] + part]
+            store(at, (total[0] - total[1]).astype(BF16), total[1].astype(BF16))
+            return 0
+
+        lax.fori_loop(0, half // TILE, tile, 0)
+
+    def squares(core, l, whole):
+        def store(at, first, second):
             out = pl.ds(pl.multiple_of(l * half + at, TILE), TILE)
-            d_v[core, out, :] = (total[0] - total[1]).astype(BF16)
-            d_v[2 + core, out, :] = total[1].astype(BF16)
-            return 0
-
-        lax.fori_loop(0, half // TILE, tile, 0)
+            d_v[core, out, :] = first
+            d_v[2 + core, out, :] = second
+            if whole:
+                out = pl.ds(pl.multiple_of(e * half + at, TILE), TILE)
+                d0_v[l, out, :] = first
+                d0_v[2 + l, out, :] = second
+
+        square_sums(m_v.at[pl.ds(2 * core, 2)], 2 * core + l, l, w_v, store)
+
+    def squares_other_rows(l):
+        def store(at, first, second):
+            out = pl.ds(pl.multiple_of(other * half + at, TILE), TILE)
+            d0_v[l, out, :] = first
+            d0_v[2 + l, out, :] = second
+
+        square_sums(mo_v, 2 * e + l, l, wo_v, store)
 
     local[4].wait()
+    local[9].wait()
     for l in range(2):
-        squares(e, l)
+        squares(e, l, True)
+        squares_other_rows(l)
 
     gains_sib.wait_recv()
     for s in range(2):
@@ -279,6 +300,7 @@
                 for k in range(2):
                     at = k * 8 + x * 4 + s * 2 + l
                     g_r[at : at + 1, :] = gin_r[s, x, l, k : k + 1, lanes]
+                    g_f[at : at + 1, :] = gin_r[s, x, l, k : k + 1, :]
     local[5].wait()
 
     def widen(pairs):
@@ -304,14 +326,20 @@
         at8 = rows_like((8, half))
         copies = []
 
-        def send(buf, at, sems, ks, peer):
-            for k in ks:
-                cp = remote(
+        def to_all(buf, at, sems, ks, peer):
+            made = [
+                remote(
                     buf.at[step, at], buf.at[step, at], sems[0].at[step, k],
                     sems[1].at[step, at], peer(k),
                 )
+                for k in ks
+            ]
+            copies.extend(made)
+            return made
+
+        def send(*args):
+            for cp in to_all(*args):
                 cp.start()
-                copies.append(cp)
 
         def gathered(buf, sems, at, count, ks, peer):
             for k in ks:
@@ -354,14 +382,33 @@
                         )
             rowd[step, c] = den_r
             send(rowd, c, (rd_s, rd_r), col_list, col_peer)
-            if short:
-                den_16 = den_c.astype(BF16)
-                colds[step, r] = jnp.concatenate([den_16[:, :half], den_16[:, half:]], axis=0)
-                send(colds, r, (cd_s, cd_r), row_list, row_peer)
-                return den_c - den_16.astype(F32)
             cold[step, r] = den_c
             send(cold, r, (cd_s, cd_r), row_list, row_peer)
-            return None
+
+        def folded(x):
+            return jnp.concatenate([x[0:4, :half], x[0:4, half:]], axis=0)
+
+        def first_denominators():
+            def own(sq):
+                rows = [
+                    jnp.where(e == 0, sq[4 * k : 4 * k + 2], sq[4 * k + 2 : 4 * k + 4])
+                    for k in range(2)
+                ]
+                return jnp.concatenate(rows + [jnp.zeros_like(sq[0:4])], axis=0).astype(BF16)
+
+            s_r, s_c = own(squared(g_f[...])), own(squared(gc))
+            at = rows_like((8, 2 * half))
+            den_c = jnp.zeros((8, 2 * half), F32)
+            den_r = jnp.zeros((8, 2 * half), F32)
+            for i in range(4):
+                part = d0_v[i]
+                got = jnp.dot(s_r, part, preferred_element_type=F32)
+                den_c = jnp.where(at == i, got, den_c)
+                den_r = jnp.where(at == i, across(s_c, part), den_r)
+            rowds[step, c] = folded(den_r)
+            colds[step, r] = folded(den_c)
+            made = to_all(rowds, c, (rd_s, rd_r), col_list, col_peer)
+            return made + to_all(colds, r, (cd_s, cd_r), row_list, row_peer)
 
         def channel(ch, _):
             if step == 0:
@@ -392,15 +439,25 @@
                     out = jnp.where(keep, product(t_v[last[k, d], d]), out)
             return out
 
-        if step > 0:
+        outer_products(a_v, gr, gc)
+        if short:
+            first = first_denominators()
+
+            @pl.when(jnp.logical_not(holder))
+            def _():
+                for cp in first:
+                    cp.start()
+
+        else:
             denominators()
-        outer_products(a_v, gr, gc)
         lax.fori_loop(0, chans, channel, 0)
-        if step == 0:
+        if short:
 
             @pl.when(holder)
             def _():
                 pl.semaphore_wait(late, len(partners) - 2)
+                for cp in first:
+                    cp.start()
 
         x_row = gc.astype(BF16)
         x_col = jnp.concatenate([gr, turned(gr)], axis=1).astype(BF16)
@@ -416,14 +473,23 @@
         if short:
             colns[step, r] = o_col.astype(BF16)
             send(colns, r, (cn_s, cn_r), row_list, row_peer)
+            dens[e] = jnp.concatenate(
+                [
+                    gathered(colds, (cd_s, cd_r), r, n_row, row_list, row_peer),
+                    gathered(rowds, (rd_s, rd_r), c, n_col, col_list, col_peer),
+                ],
+                axis=0,
+            )
+            dens_sib = remote(dens.at[e], dens.at[e], ds_s, ds_r.at[e], sib)
+            dens_sib.start()
+            copies.append(dens_sib)
             for l in range(2):
-                squares(other, l)
-            lost_den = denominators()
+                squares(other, l, False)
             lax.fori_loop(0, chans, widen_model, 0)
         else:
             coln[step, r] = o_col + error[1]
             send(coln, r, (cn_s, cn_r), row_list, row_peer)
-            for cp in local[6:]:
+            for cp in local[6:8]:
                 cp.wait()
             remote(
                 model.at[:, :, their_ch, mine, :], mf_v.at[pl.ds(2 * other, 2)],
@@ -437,9 +503,22 @@
             return 0.5 * total / den
 
         total = gathered(colns if short else coln, (cn_s, cn_r), r, n_row, row_list, row_peer)
-        total_den = gathered(colds if short else cold, (cd_s, cd_r), r, n_row, row_list, row_peer)
         if short:
-            total_den = jnp.concatenate([total_den[0:8], total_den[8:16]], axis=1)
+            remote(dens.at[other], dens.at[other], ds_s, ds_r.at[other], sib).wait_recv()
+            cores = []
+            for i in range(2):
+                part = dens[i]
+                cores.append((
+                    jnp.concatenate([part[0:4], part[4:8]], axis=1),
+                    jnp.where(e == 0, part[8:12], part[12:16]),
+                ))
+            den_c, den_r = (
+                jnp.concatenate([x[0:2], y[0:2], x[2:4], y[2:4]], axis=0)
+                for x, y in zip(*cores)
+            )
+            total_den = jnp.zeros((8, 2 * half), F32)
+        else:
+            total_den = gathered(cold, (cd_s, cd_r), r, n_row, row_list, row_peer)
         colt[step, e] = jnp.concatenate([total, total_den], axis=0)
         both = remote(
             colt.at[step, e], colt.at[step, e], ct_s.at[step], ct_r.at[step, e], sib
@@ -447,8 +526,9 @@
         both.start()
         copies.append(both)
         total = gathered(rowns if short else rown, (rn_s, rn_r), c, n_col, col_list, col_peer)
-        total_den = gathered(rowd, (rd_s, rd_r), c, n_col, col_list, col_peer)
-        change_r = refresh(total, total_den)
+        if not short:
+            den_r = gathered(rowd, (rd_s, rd_r), c, n_col, col_list, col_peer)
+        change_r = refresh(total, den_r)
         g_r[...] = gr + change_r
         if step == ITERS - 1:
             g_r2[e] = g_r[...]
@@ -459,15 +539,12 @@
             colt.at[step, other], colt.at[step, other], ct_s.at[step], ct_r.at[step, other], sib
         ).wait_recv()
         total = colt[step, 0] + colt[step, 1]
-        change_c = refresh(total[0:16], total[16:24])
+        change_c = refresh(total[0:16], den_c if short else total[16:24])
         g_c[...] = gc + change_c
         if short:
             lost_r = o_row - rowns[step, c].astype(F32)
             lost_c = o_col - colns[step, r].astype(F32)
-            lost_den = jnp.concatenate(
-                [lost_den[0:4], lost_den[0:4], lost_den[4:8], lost_den[4:8]], axis=0
-            )
-            error = (0.5 * lost_r, 0.5 * lost_c - change_c * lost_den)
+            error = (0.5 * lost_r, 0.5 * lost_c)
         return copies, error
 
     copies, error = [], None
@@ -494,7 +571,7 @@
         cp.wait_send()
 
 
-def finish_kernel(m_w, mf_w, v_w, g_r2, g_c, idx, gains_out, res_out, a_v, out_v, g_v, sem, g_sem):
+def finish_kernel(m_w, mf_w, v_w, g_r2, g_c, idx, gains_out, res_out, a_v, b_v, out_v, g_v, sem, g_sem):
     e = lax.axis_index("dir")
     half = m_w.shape[3]
     fin = mf_w.shape[2]
@@ -518,14 +595,16 @@
             out_v.at[which, :, ch], res_out.at[:, ch, where, :], sem.at[which, ch]
         )
 
+    products = (a_v, b_v)
+    for which in range(2):
+        outer_products(products[which], g_r2[sides[which][3]], g)
     for which, (mod, vi, base, side) in enumerate(sides):
-        outer_products(a_v.at[which], g_r2[side], g)
 
         for ch in range(fin):
             picks = [idx[d, e * fin + ch] for d in range(4)]
             for t in range(half // TILE):
                 rows = slice(t * TILE, (t + 1) * TILE)
-                re, im = residual_tile(a_v.at[which], mod, vi, base + ch, picks, rows, ch)
+                re, im = residual_tile(products[which], mod, vi, base + ch, picks, rows, ch)
                 out_v[which, 0, ch, rows, :] = re
                 out_v[which, 1, ch, rows, :] = im
             moved(which, ch).start()
@@ -567,10 +646,14 @@
             pltpu.VMEM((2, chans, half, cols), BF16),
             pltpu.VMEM((n_dir, 2, fin, half, cols), BF16),
             pltpu.VMEM((2, fin, half, cols), BF16),
+            pltpu.VMEM((2, 2, chans, half, cols), BF16),
             pltpu.VMEM((chans, half, cols), BF16),
+            pltpu.VMEM((chans, half, cols), BF16),
+            pltpu.VMEM((4, 2 * half, cols), BF16),
             pltpu.VMEM((4, 2 * half, cols), BF16),
             pltpu.VMEM((8, half, 2 * cols), F32),
             pltpu.VMEM((chans + 1, n_dir, 2 * half, cols), BF16),
+            pltpu.VMEM((chans, half), jnp.int32),
             pltpu.VMEM((chans, half), jnp.int32),
             pltpu.VMEM((chans, cols), jnp.int32),
             pltpu.SMEM((n_dir, chans), jnp.int32),
@@ -583,11 +666,14 @@
             pltpu.VMEM((ITERS, n_col, 16, half), F32),
             pltpu.VMEM((ITERS, n_col, 8, half), F32),
             pltpu.VMEM((1, n_row, 16, cols), BF16),
-            pltpu.VMEM((1, n_row, 16, half), BF16),
+            pltpu.VMEM((1, n_row, 8, half), F32),
             pltpu.VMEM((1, n_col, 16, half), BF16),
+            pltpu.VMEM((1, n_col, 8, half), F32),
+            pltpu.VMEM((2, 16, half), F32),
+            pltpu.VMEM((16, cols), F32),
             pltpu.VMEM((ITERS, 2, 24, cols), F32),
             pltpu.SemaphoreType.REGULAR,
-            dma((8,)),
+            dma((10,)),
             dma((chans + 1,)),
             dma((chans + 1,)),
             dma,
@@ -606,9 +692,11 @@
             dma((ITERS, 2)),
             dma,
             dma((2,)),
+            dma,
+            dma((2,)),
         ],
         compiler_params=pltpu.CompilerParams(
-            collective_id=0, has_side_effects=True, vmem_limit_bytes=28 * 2**20
+            collective_id=0, has_side_effects=True, vmem_limit_bytes=32 * 2**20
         ),
     )(*args)
     return pl.pallas_call(
@@ -620,7 +708,8 @@
         in_specs=spaces,
         out_specs=(hbm, hbm),
         scratch_shapes=[
-            pltpu.VMEM((2, 8, half, 2 * cols), F32),
+            pltpu.VMEM((8, half, 2 * cols), F32),
+            pltpu.VMEM((8, half, 2 * cols), F32),
             pltpu.VMEM((2, 2, fin, half, cols), F32),
             pltpu.VMEM(gains.shape, F32),
             dma((2, fin)),

time: 35 us -> 34.7 us (level)
  no operation moved by 1% of the time
where the time goes in v6:
time: 34.7 us; the launch traced here: 34.6 us
  Pallas kernels  34 us (98%)
  between operations  0.64 us (2%)
    pallas_call x1, Pallas kernels, body(): pl.pallas_call(functools.partial(kernel, n_row, n_col), out_shape=held, i...  31.5 us
    pallas_call x1, Pallas kernels, body(): pl.pallas_call(finish_kernel, out_shape=(pltpu.HBM(gains.shape, F32), plt...  2.45 us

profile of v6, /device:TPU:1, one launch (start us, length us, event | category | flops | bytes accessed | tf_op | source)
XLA Modules:
  0.0 34.6 jit_solution(5727892530810647331)
XLA Ops:
  0.6 31.5 %shard_map.68 = (f32[4,2,8,128,256]{4,3,2,1,0:T(8,128)S(1)}, f32[4,2,4,128,256]{4,3,2,1,0:T(8,128)S(1)}, f32[2,2,4,128,256]{4,3,2,1,0:T(8,128)S(1)}, f32[2,16,12...) custom-call(bf16[2,8,256,256]{3,2,1,0:T(8,128)(2,1)} %vis.1, bf16[2,2,8,256,256]{4,3,2,1,0:T(8,128)(2,1)} %model.1, ...), custom_call_target="tpu_custom_call" | custom-call | tf_op jit(solution)/shard_map/pallas_call | solution.py:639
  32.1 2.4 %shard_map.69 = (f32[2,2,2,256]{3,2,1,0:T(2,128)}, f32[2,4,256,256]{3,2,1,0:T(8,128)}) custom-call(f32[4,2,8,128,256]{4,3,2,1,0:T(8,128)S(1)} %get-tuple-element.8.m_w, f32[4,2,4,128,256]{4,3,2,1,0:T(8,128)S(1)} %get-tuple-element.9.mf_w, f32[2,2,4,128,256]{4,3,2,1,0:T(8,128)S(1)} %get-tuple-element.10.v_w, f32[2,16,128]{2,1,0:T(8,128)S(1)} %get-tuple-element.11.g_r2, ...), custom_call_target="tpu_custom_call" | custom-call | tf_op jit(solution)/shard_map/pallas_call | solution.py:702

commit v7 on v6

--- a/solution.py
+++ b/solution.py
@@ -473,6 +473,9 @@
         if short:
             colns[step, r] = o_col.astype(BF16)
             send(colns, r, (cn_s, cn_r), row_list, row_peer)
+            for l in range(2):
+                squares(other, l, False)
+            lax.fori_loop(0, chans, widen_model, 0)
             dens[e] = jnp.concatenate(
                 [
                     gathered(colds, (cd_s, cd_r), r, n_row, row_list, row_peer),
@@ -483,9 +486,6 @@
             dens_sib = remote(dens.at[e], dens.at[e], ds_s, ds_r.at[e], sib)
             dens_sib.start()
             copies.append(dens_sib)
-            for l in range(2):
-                squares(other, l, False)
-            lax.fori_loop(0, chans, widen_model, 0)
         else:
             coln[step, r] = o_col + error[1]
             send(coln, r, (cn_s, cn_r), row_list, row_peer)

time: 34.7 us -> 34.5 us (level)
  no operation moved by 1% of the time
where the time goes in v7:
time: 34.5 us; the launch traced here: 34.4 us
  Pallas kernels  33.8 us (98%)
  between operations  0.64 us (2%)
    pallas_call x1, Pallas kernels, body(): pl.pallas_call(functools.partial(kernel, n_row, n_col), out_shape=held, i...  31.3 us
    pallas_call x1, Pallas kernels, body(): pl.pallas_call(finish_kernel, out_shape=(pltpu.HBM(gains.shape, F32), plt...  2.45 us

profile of v7, /device:TPU:1, one launch (start us, length us, event | category | flops | bytes accessed | tf_op | source)
XLA Modules:
  0.0 34.4 jit_solution(10536656276834317497)
XLA Ops:
  0.6 31.3 %shard_map.68 = (f32[4,2,8,128,256]{4,3,2,1,0:T(8,128)S(1)}, f32[4,2,4,128,256]{4,3,2,1,0:T(8,128)S(1)}, f32[2,2,4,128,256]{4,3,2,1,0:T(8,128)S(1)}, f32[2,16,12...) custom-call(bf16[2,8,256,256]{3,2,1,0:T(8,128)(2,1)} %vis.1, bf16[2,2,8,256,256]{4,3,2,1,0:T(8,128)(2,1)} %model.1, ...), custom_call_target="tpu_custom_call" | custom-call | tf_op jit(solution)/shard_map/pallas_call | solution.py:639
  32.0 2.4 %shard_map.69 = (f32[2,2,2,256]{3,2,1,0:T(2,128)}, f32[2,4,256,256]{3,2,1,0:T(8,128)}) custom-call(f32[4,2,8,128,256]{4,3,2,1,0:T(8,128)S(1)} %get-tuple-element.8.m_w, f32[4,2,4,128,256]{4,3,2,1,0:T(8,128)S(1)} %get-tuple-element.9.mf_w, f32[2,2,4,128,256]{4,3,2,1,0:T(8,128)S(1)} %get-tuple-element.10.v_w, f32[2,16,128]{2,1,0:T(8,128)S(1)} %get-tuple-element.11.g_r2, ...), custom_call_target="tpu_custom_call" | custom-call | tf_op jit(solution)/shard_map/pallas_call | solution.py:702
